TPU v7x, 256 devices: a whole 4x4x8 slice. The times are simulated.
256 devices in a mesh: bucket: 32 (over y, z), col: 8 (over x, core).
Axes of the slice: x: 4, y: 4, z: 8, core: 2. Of those that a mesh axis runs over, the one named last changes fastest.
Arguments:
- entity_table: bfloat16 [262144, 1024], P('bucket', 'col'), may hold values from -9 to 9
- relation_table: bfloat16 [4096, 1024], P(None, 'col'), may hold values from -4 to 4
- head_row: int32 [65536], P('bucket'), may hold values from 0 to 8191
- relation_id: int32 [65536], P('bucket'), may hold values from 0 to 4095
- tail_owner: int32 [65536, 1], P('bucket'), may hold values from 0 to 31; in each aligned block of 2048 rows (0 to 2047, 2048 to 4095, ...) at most 128 rows name the same one
- tail_row: int32 [65536], P('bucket'), may hold values from 0 to 8191
- negative_row: int32 [128, 1000], P('bucket'), may hold values from 0 to 8191
Outputs:
- loss: float32 [65536], P('bucket')
- entity_grad: float32 [262144, 1024], P('bucket', 'col')
- relation_grad: float32 [4096, 1024], P('bucket', 'col')
Inputs may be any that keep to these rules, and one draw needn't show every extreme that they name: `tail_owner`: in the 2048 edges of one bucket group no partition is named more than 128 times, a bound that some block reaches.
All inputs are finite; a program needn't handle non-finite values.
Results may differ from a plain program's by a relative error of at most 0.0061.
Values may be sent and summed in bfloat16 or wider, within the bound.
A program may use at most 64 MiB of HBM per device.

v0:
```python
import jax
import jax.numpy as jnp
from jax import lax
from jax.sharding import PartitionSpec as P

PAIR = 128
SPAN = 512


def complex_mul(left, right, sign):
    shape = left.shape
    first = left.reshape(shape[:-1] + (-1, 2, PAIR // 2))
    second = right.reshape(shape[:-1] + (-1, 2, PAIR // 2))
    left_re = first[..., 0, :]
    left_im = first[..., 1, :]
    right_re = second[..., 0, :]
    right_im = sign * second[..., 1, :]
    real_part = left_re * right_re - left_im * right_im
    imag_part = left_re * right_im + left_im * right_re
    return jnp.stack([real_part, imag_part], axis=-2).reshape(shape)


def body(entity_table, relation_table, head_row, relation_id, tail_owner, tail_row, negative_row):
    buckets = lax.axis_size("bucket")
    edges = head_row.shape[0]
    width = entity_table.shape[1]
    capacity = 2 * edges // buckets
    owner = tail_owner[:, 0]
    matches = (owner[:, None] == jnp.arange(buckets, dtype=jnp.int32)[None, :]).astype(jnp.int32)
    rank = jnp.sum((jnp.cumsum(matches, axis=0) - 1) * matches, axis=1)
    target = owner * capacity + rank
    request = jnp.zeros((buckets * capacity,), jnp.int32).at[target].set(tail_row)
    request = request.reshape(buckets, capacity)
    asked = lax.all_to_all(request, "bucket", split_axis=0, concat_axis=0, tiled=True)
    found = entity_table[asked]
    fetched = lax.all_to_all(found, "bucket", split_axis=0, concat_axis=0, tiled=True)
    tail_emb = fetched.reshape(buckets * capacity, width)[target]
    head_emb = entity_table[head_row].astype(jnp.float32)
    rel_emb = relation_table[relation_id].astype(jnp.float32)
    product = complex_mul(head_emb, rel_emb, 1.0).astype(jnp.bfloat16)
    partial_pos = jnp.sum(product.astype(jnp.float32) * tail_emb.astype(jnp.float32), axis=1)
    positive = lax.psum(partial_pos, "col")

    def span_step(grad, inputs):
        prod, pos, negs = inputs
        neg_emb = entity_table[negs]
        partial_value = jnp.dot(prod, neg_emb.T, preferred_element_type=jnp.float32)
        scores = lax.psum(partial_value, "col")
        top = jnp.maximum(jnp.max(scores, axis=1), pos)
        expo = jnp.exp(scores - top[:, None])
        expo_pos = jnp.exp(pos - top)
        total = jnp.sum(expo, axis=1) + expo_pos
        weight = (expo / total[:, None]).astype(jnp.bfloat16)
        loss = top + jnp.log(total) - pos
        pos_grad = expo_pos / total - 1.0
        prod_grad = jnp.dot(weight, neg_emb, preferred_element_type=jnp.float32)
        neg_grad = lax.dot_general(
            weight, prod, (((0,), (0,)), ((), ())), preferred_element_type=jnp.float32
        )
        grad = grad.at[negs].add(neg_grad)
        return (grad, (loss, prod_grad, pos_grad))

    spans = edges // SPAN
    start = jnp.zeros((entity_table.shape[0], width), jnp.float32)
    inputs = (product.reshape(spans, SPAN, width), positive.reshape(spans, SPAN), negative_row)
    grad, (loss, prod_grad, pos_grad) = lax.scan(span_step, start, inputs)
    loss = loss.reshape(edges)
    pos_grad = pos_grad.reshape(edges)
    prod_grad = prod_grad.reshape(edges, width) + pos_grad[:, None] * tail_emb.astype(jnp.float32)
    head_grad = complex_mul(prod_grad, rel_emb, -1.0)
    rel_grad = complex_mul(prod_grad, head_emb, -1.0)
    grad = grad.at[head_row].add(head_grad)
    tail_grad = pos_grad[:, None] * product.astype(jnp.float32)
    outgoing = jnp.zeros((buckets * capacity, width), jnp.float32).at[target].set(tail_grad)
    incoming = lax.all_to_all(
        outgoing.reshape(buckets, capacity, width),
        "bucket",
        split_axis=0,
        concat_axis=0,
        tiled=True,
    )
    grad = grad.at[asked.reshape(-1)].add(incoming.reshape(buckets * capacity, width))
    rel_local = (
        jnp.zeros((relation_table.shape[0], width), jnp.float32).at[relation_id].add(rel_grad)
    )
    relation_grad = lax.psum_scatter(rel_local, "bucket", scatter_dimension=0, tiled=True)
    return (loss, grad, relation_grad)


def solution(mesh):
    in_specs = (
        P("bucket", "col"),
        P(None, "col"),
        P("bucket"),
        P("bucket"),
        P("bucket", None),
        P("bucket"),
        P("bucket", None),
    )
    out_specs = (P("bucket"), P("bucket", "col"), P("bucket", "col"))
    return jax.shard_map(body, mesh=mesh, in_specs=in_specs, out_specs=out_specs, check_vma=False)
```

profile of v0, /device:TPU:32, one launch (start us, length us, event | category | flops | bytes accessed | tf_op | source)
XLA Modules:
  0.0 786.8 jit_solution(7550381844161596740)
XLA Ops:
  9.6 15.9 %reduce-window.6 = s32[32,16,128]{2,1,0:T(8,128)S(1)} reduce-window(s32[32,16,128]{2,1,0:T(8,128)} %fusion.15, s32[]{:T(128)} %constant.67.clone.1), window={size=1x1x128 pad=0_0x0_0x127_0}, to_apply=%region_0.0 | reduce-window | flops 8323072 | bytes 524292 | tf_op jit(solution)/shard_map/reduce-window
  28.0 8.2 %scatter_custom_fusion.1 = s32[4096]{0:T(1024)S(1)} fusion(s32[2048]{0:T(1024)S(1)} %bitcast.123, s32[2048]{0:T(1024)} %param.14, s32[]{:T(128)} %constant.67.clone.1), kind=kCustom, calls=%fused_computation.61 | custom fusion | bytes 16896 | tf_op jit(solution)/shard_map/scatter | solution.py:32
  36.2 19.8 %all_to_all.22 = s32[32,1,128]{2,1,0:T(1,128)S(1)} all-to-all(s32[32,1,128]{2,1,0:T(1,128)S(1)} %bitcast.121), channel_id=1, replica_groups=mesh['bucket'=32,'col'=8] {'bucket'}, dimensions={0} | all-to-all | bytes 32768 | tf_op jit(solution)/shard_map/all_to_all | solution.py:34
  56.0 14.9 %gather_fusion.3 = bf16[4096,128]{1,0:T(8,128)(2,1)} fusion(bf16[8192,128]{1,0:T(8,128)(2,1)S(1)} %copy-done.2, s32[4096]{0:T(1024)S(1)} %fusion.17), kind=kCustom, calls=%fused_computation.3 | custom fusion | bytes 2113536 | tf_op jit(solution)/shard_map/gather | solution.py:35
  70.9 5.8 all-to-all-start.1
  76.8 8.1 %gather_fusion.2 = bf16[2048,128]{1,0:T(8,128)(2,1)} fusion(bf16[4096,128]{1,0:T(8,128)(2,1)S(1)} %copy-done, s32[2048]{0:T(1024)S(1)} %get-tuple-element.161), kind=kCustom, calls=%fused_computation.2 | custom fusion | bytes 1056768 | tf_op jit(solution)/shard_map/gather | solution.py:39
  84.8 2.2 copy.11
  87.1 8.1 %gather_fusion.1 = bf16[2048,128]{1,0:T(8,128)(2,1)} fusion(bf16[8192,128]{1,0:T(8,128)(2,1)S(1)} %copy-done.2, s32[2048]{0:T(1024)S(1)} %get-tuple-element.163), kind=kCustom, calls=%fused_computation.1 | custom fusion | bytes 1056768 | tf_op jit(solution)/shard_map/gather | solution.py:38
  95.1 2.2 copy.10
  99.9 2.2 convert_element_type.95
  102.1 2.3 copy.15
  106.6 2.6 copy.14
  109.2 9.1 %gather_fusion.4 = bf16[2048,128]{1,0:T(8,128)(2,1)} fusion(bf16[4096,128]{1,0:T(8,128)(2,1)} %bitcast.21, s32[2048]{0:T(1024)S(1)} %broadcast_clamp_fusion), kind=kCustom, calls=%fused_computation.4 | custom fusion | bytes 1056768 | tf_op jit(solution)/shard_map/gather | solution.py:37
  118.2 2.2 copy.17
  122.2 13.2 %psum.17 = f32[4,512]{1,0:T(4,128)S(1)} all-reduce(f32[4,512]{1,0:T(4,128)S(1)} %reshape.353), channel_id=1, replica_groups=mesh['bucket'=32,'col'=8] {'col'}, use_global_device_ids=true, to_apply=%region_5.6 | all-reduce | flops 2048 | bytes 16384 | tf_op jit(solution)/shard_map/psum | solution.py:42
  135.3 2.3 broadcast_in_dim.22
  137.6 395.6 %while.18 = (s32[]{:T(128)}, f32[8192,128]{1,0:T(8,128)}, f32[4,512]{1,0:T(4,128)S(1)}, f32[4,512,128]{1,0,2:T(4,128)}, f32[4,512]{1,0:T(4,128)S(1)}, /*index=5*...) while((s32[]{:T(128)}, f32[8192,128]{1,0:T(8,128)}, ...), condition=%wide.region_11.12_spmd, body=%wide.region_6.0_spmd.sunk | while | flops 396936128 | bytes 44848936 | solution.py:66
  138.4 3.3 gather_fusion
  141.7 2.7 fusion.39
  144.4 69.6 %all-reduce.2.cloned.1.call-done = f32[512,1000]{0,1:T(8,128)} async-done(((f32[512,1000]{0,1:T(8,128)}), f32[512,1000]{0,1:T(8,128)}) %all-reduce.2.cloned.1.call-update) | async-done | bytes 2048016 | tf_op jit(solution)/shard_map/while/body/eval_jaxpr/psum | solution.py:48
  217.4 2.1 fusion.41
  219.8 6.1 dynamic_update_slice.24
  225.9 10.2 %scatter_fusion = f32[8192,128]{1,0:T(8,128)} fusion(f32[8192,128]{1,0:T(8,128)} %get-tuple-element.238, s32[1000]{0:T(1024)S(1)} %bitcast.108, f32[1000,128]{1,0:T(8,128)} %fusion.41), kind=kCustom, calls=%fused_computation.5.clone.1 | custom fusion | flops 128000 | bytes 1540000 | tf_op jit(solution)/shard_map/while/body/eval_jaxpr/scatter-add | solution.py:60
  236.8 3.3 gather_fusion
  240.2 2.7 fusion.39
  242.8 70.2 %all-reduce.2.cloned.1.call-done = f32[512,1000]{0,1:T(8,128)} async-done(((f32[512,1000]{0,1:T(8,128)}), f32[512,1000]{0,1:T(8,128)}) %all-reduce.2.cloned.1.call-update) | async-done | bytes 2048016 | tf_op jit(solution)/shard_map/while/body/eval_jaxpr/psum | solution.py:48
  316.4 2.1 fusion.41
  318.9 6.1 dynamic_update_slice.24
  325.0 10.2 %scatter_fusion = f32[8192,128]{1,0:T(8,128)} fusion(f32[8192,128]{1,0:T(8,128)} %get-tuple-element.238, s32[1000]{0:T(1024)S(1)} %bitcast.108, f32[1000,128]{1,0:T(8,128)} %fusion.41), kind=kCustom, calls=%fused_computation.5.clone.1 | custom fusion | flops 128000 | bytes 1540000 | tf_op jit(solution)/shard_map/while/body/eval_jaxpr/scatter-add | solution.py:60
  335.9 3.3 gather_fusion
  339.2 2.7 fusion.39
  341.9 70.2 %all-reduce.2.cloned.1.call-done = f32[512,1000]{0,1:T(8,128)} async-done(((f32[512,1000]{0,1:T(8,128)}), f32[512,1000]{0,1:T(8,128)}) %all-reduce.2.cloned.1.call-update) | async-done | bytes 2048016 | tf_op jit(solution)/shard_map/while/body/eval_jaxpr/psum | solution.py:48
  417.9 6.1 dynamic_update_slice.24
  424.0 10.2 %scatter_fusion = f32[8192,128]{1,0:T(8,128)} fusion(f32[8192,128]{1,0:T(8,128)} %get-tuple-element.238, s32[1000]{0:T(1024)S(1)} %bitcast.108, f32[1000,128]{1,0:T(8,128)} %fusion.41), kind=kCustom, calls=%fused_computation.5.clone.1 | custom fusion | flops 128000 | bytes 1540000 | tf_op jit(solution)/shard_map/while/body/eval_jaxpr/scatter-add | solution.py:60
  435.0 3.3 gather_fusion
  438.3 2.7 fusion.39
  441.0 70.2 %all-reduce.2.cloned.1.call-done = f32[512,1000]{0,1:T(8,128)} async-done(((f32[512,1000]{0,1:T(8,128)}), f32[512,1000]{0,1:T(8,128)}) %all-reduce.2.cloned.1.call-update) | async-done | bytes 2048016 | tf_op jit(solution)/shard_map/while/body/eval_jaxpr/psum | solution.py:48
  517.0 6.1 dynamic_update_slice.24
  523.1 10.2 %scatter_fusion = f32[8192,128]{1,0:T(8,128)} fusion(f32[8192,128]{1,0:T(8,128)} %get-tuple-element.238, s32[1000]{0:T(1024)S(1)} %bitcast.108, f32[1000,128]{1,0:T(8,128)} %fusion.41), kind=kCustom, calls=%fused_computation.5.clone.1 | custom fusion | flops 128000 | bytes 1540000 | tf_op jit(solution)/shard_map/while/body/eval_jaxpr/scatter-add | solution.py:60
  533.3 2.9 reshape.355
  540.2 12.9 %scatter_custom_fusion.5 = f32[4096,128]{1,0:T(8,128)} fusion(s32[2048]{0:T(1024)S(1)} %get-tuple-element.160, f32[2048,128]{1,0:T(8,128)S(1)} %copy.20, f32[]{:T(128)} %constant.68.clone.1), kind=kCustom, calls=%fused_computation.33 | custom fusion | flops 262144 | bytes 2097156 | tf_op jit(solution)/shard_map/scatter-add | solution.py:84
  554.6 7.3 scatter_custom_fusion.3
  561.9 10.1 %all-to-all-start.2 = ((f32[32,128,128]{2,1,0:T(8,128)}), f32[32,128,128]{2,1,0:T(8,128)S(1)}, u32[]{:S(2)}, u32[]{:S(2)}) async-start(f32[32,128,128]{2,1,0:T(8,128)} %bitcast.101), calls=%async_computation.2 | async-start | bytes 4194304 | tf_op jit(solution)/shard_map/all_to_all | solution.py:75
  572.6 2.6 copy.18
  575.2 14.9 %scatter_fusion.1 = f32[8192,128]{1,0:T(8,128)} fusion(f32[8192,128]{1,0:T(8,128)} %get-tuple-element.265, s32[2048]{0:T(1024)S(1)} %get-tuple-element.162, f32[2048,128]{1,0:T(8,128)} %copy.18), kind=kCustom, calls=%fused_computation.7 | custom fusion | flops 262144 | bytes 3153920 | tf_op jit(solution)/shard_map/scatter-add | solution.py:72
  590.1 34.0 %all-to-all-done.2 = f32[32,128,128]{2,1,0:T(8,128)S(1)} async-done(((f32[32,128,128]{2,1,0:T(8,128)}), f32[32,128,128]{2,1,0:T(8,128)S(1)}, u32[]{:S(2)}, u32[]{:S(2)}) %all-to-all-start.2) | async-done | bytes 2097184 | tf_op jit(solution)/shard_map/all_to_all | solution.py:75
  624.1 24.8 %scatter_fusion.2 = f32[8192,128]{1,0:T(8,128)} fusion(f32[8192,128]{1,0:T(8,128)} %scatter_fusion.1, s32[4096]{0:T(1024)S(1)} %bitcast.118, f32[4096,128]{1,0:T(8,128)S(1)} %bitcast.100), kind=kCustom, calls=%fused_computation.9 | custom fusion | flops 524288 | bytes 6307840 | tf_op jit(solution)/shard_map/scatter-add | solution.py:82
  648.9 130.8 %reduce-scatter.2.cloned.1.call-done = f32[128,128]{1,0:T(8,128)} async-done(((f32[4096,128]{1,0:T(8,128)}), f32[128,128]{1,0:T(8,128)}) %reduce-scatter.2.cloned.1.call-update) | async-done | bytes 65552 | tf_op jit(solution)/shard_map/reduce_scatter | solution.py:86
  (125 shorter events, 38.4 us)
Async XLA Ops:
  8.0 68.8 %copy-start = (bf16[4096,128]{1,0:T(8,128)(2,1)S(1)}, bf16[4096,128]{1,0:T(8,128)(2,1)}, u32[]{:S(2)}) copy-start(bf16[4096,128]{1,0:T(8,128)(2,1)} %param.10) | copy-start | bytes 3145732
  8.0 19.8 %copy-start.7 = (s32[2048,1]{0,1:T(1,128)S(1)}, s32[2048,1]{0,1:T(1,128)}, u32[]{:S(2)}) copy-start(s32[2048,1]{0,1:T(1,128)} %param.13) | copy-start | bytes 24580
  8.0 48.0 %copy-start.2 = (bf16[8192,128]{1,0:T(8,128)(2,1)S(1)}, bf16[8192,128]{1,0:T(8,128)(2,1)}, u32[]{:S(2)}) copy-start(bf16[8192,128]{1,0:T(8,128)(2,1)} %param.9) | copy-start | bytes 6291460
  70.9 5.8 copy-start.8
  70.9 38.2 %all-to-all-start.1 = ((bf16[32,128,128]{2,1,0:T(8,128)(2,1)}), bf16[32,128,128]{2,1,0:T(8,128)(2,1)}, u32[]{:S(2)}, u32[]{:S(2)}) async-start(bf16[32,128,128]{2,1,0:T(8,128)(2,1)} %bitcast.103), calls=%async_computation.1 | async-start | bytes 2097152 | tf_op jit(solution)/shard_map/all_to_all | solution.py:36
  76.8 10.3 %copy-start.9 = (s32[2048]{0:T(1024)S(1)}, s32[2048]{0:T(1024)}, u32[]{:S(2)}) copy-start(s32[2048]{0:T(1024)} %param.11) | copy-start | bytes 24580
  137.6 76.3 %all-reduce.2.cloned.1.call-start = ((), (), s32[]{:S(2)}) async-start(), calls=%async_computation.5 | async-start | bytes 4096000 | tf_op jit(solution)/shard_map/while/body/eval_jaxpr/psum | solution.py:48
  214.0 2.2 copy-start.1
  225.9 10.2 %copy-start.3 = (bf16[8192,128]{1,0:T(8,128)(2,1)S(1)}, bf16[8192,128]{1,0:T(8,128)(2,1)}, u32[]{:S(2)}) copy-start(bf16[8192,128]{1,0:T(8,128)(2,1)} %get-tuple-element.276) | copy-start | bytes 6291460 | tf_op jit(solution)/shard_map/while
  236.1 77.0 %all-reduce.2.cloned.1.call-start = ((), (), s32[]{:S(2)}) async-start(), calls=%async_computation.5 | async-start | bytes 4096000 | tf_op jit(solution)/shard_map/while/body/eval_jaxpr/psum | solution.py:48
  313.0 2.2 copy-start.1
  324.9 10.2 %copy-start.3 = (bf16[8192,128]{1,0:T(8,128)(2,1)S(1)}, bf16[8192,128]{1,0:T(8,128)(2,1)}, u32[]{:S(2)}) copy-start(bf16[8192,128]{1,0:T(8,128)(2,1)} %get-tuple-element.276) | copy-start | bytes 6291460 | tf_op jit(solution)/shard_map/while
  335.1 77.0 %all-reduce.2.cloned.1.call-start = ((), (), s32[]{:S(2)}) async-start(), calls=%async_computation.5 | async-start | bytes 4096000 | tf_op jit(solution)/shard_map/while/body/eval_jaxpr/psum | solution.py:48
  412.1 2.2 copy-start.1
  424.0 10.2 %copy-start.3 = (bf16[8192,128]{1,0:T(8,128)(2,1)S(1)}, bf16[8192,128]{1,0:T(8,128)(2,1)}, u32[]{:S(2)}) copy-start(bf16[8192,128]{1,0:T(8,128)(2,1)} %get-tuple-element.276) | copy-start | bytes 6291460 | tf_op jit(solution)/shard_map/while
  434.2 77.0 %all-reduce.2.cloned.1.call-start = ((), (), s32[]{:S(2)}) async-start(), calls=%async_computation.5 | async-start | bytes 4096000 | tf_op jit(solution)/shard_map/while/body/eval_jaxpr/psum | solution.py:48
  511.2 2.2 copy-start.1
  523.1 10.2 %copy-start.3 = (bf16[8192,128]{1,0:T(8,128)(2,1)S(1)}, bf16[8192,128]{1,0:T(8,128)(2,1)}, u32[]{:S(2)}) copy-start(bf16[8192,128]{1,0:T(8,128)(2,1)} %get-tuple-element.276) | copy-start | bytes 6291460 | tf_op jit(solution)/shard_map/while
  533.3 246.4 %reduce-scatter.2.cloned.1.call-start = ((), (), s32[]{:S(2)}) async-start(), calls=%async_computation.4 | async-start | bytes 2162688 | tf_op jit(solution)/shard_map/reduce_scatter | solution.py:86
  536.2 1.9 copy-start.4
  536.2 2.2 copy-start.5
  540.1 12.9 %copy-start.6 = (bf16[2048,1,2,64]{0,3,2,1:T(8,128)(2,1)S(1)}, bf16[2048,1,2,64]{0,3,2,1:T(8,128)(2,1)}, u32[]{:S(2)}) copy-start(bf16[2048,1,2,64]{0,3,2,1:T(8,128)(2,1)} %maximum_convert_fusion) | copy-start | bytes 1572868
  561.9 62.2 %all-to-all-start.2 = ((f32[32,128,128]{2,1,0:T(8,128)}), f32[32,128,128]{2,1,0:T(8,128)S(1)}, u32[]{:S(2)}, u32[]{:S(2)}) async-start(f32[32,128,128]{2,1,0:T(8,128)} %bitcast.101), calls=%async_computation.2 | async-start | bytes 4194304 | tf_op jit(solution)/shard_map/all_to_all | solution.py:75
Sparse Core Ops, SparseCore 0:
  144.5 69.4 all-reduce.1
  243.0 70.0 all-reduce.1
  342.0 70.0 all-reduce.1
  441.1 70.0 all-reduce.1
Sparse Core Ops, SparseCore 1:
  553.2 226.5 reduce-scatter.1
where the time goes:
time: 791 us; the launch traced here: 787 us
  waiting for transfers between devices  445 us (56%)
  other arithmetic  135 us (17%)
  local copies, waits for them, and re-layouts  122 us (15%)
  blocking collectives  32.9 us (4%)
  matrix products  21.1 us (3%)
  starting transfers between devices  15.9 us (2%)
  between operations  15.4 us (2%)
    psum x4, waiting for transfers between devices, span_step(): scores = lax.psum(partial_value, 'col')  280 us
    reduce_scatter x1, waiting for transfers between devices, body(): lax.psum_scatter(rel_local, 'bucket', scatter_dimension=0, tiled=True)  131 us
    scatter-add x4, other arithmetic, span_step(): grad = grad.at[negs].add(neg_grad)  40.7 us
    all_to_all x1, waiting for transfers between devices, body(): lax.all_to_all(outgoing.reshape(buckets, capacity, width), 'bucket', spli...  34 us
    dynamic_update_slice x16, local copies, waits for them, and re-layouts, body(): grad, (loss, prod_grad, pos_grad) = lax.scan(span_step, start, inputs)  25.4 us
    scatter-add x1, other arithmetic, body(): grad.at[asked.reshape(-1)].add(incoming.reshape(buckets * capacity, width))  24.8 us
    all_to_all x1, blocking collectives, body(): lax.all_to_all(request, 'bucket', split_axis=0, concat_axis=0, tiled=True)  19.8 us
    another operation x4, other arithmetic  16.1 us
  transfers between devices with their start and end apart: 7, of which 6 were waited for; matrix products, arithmetic and copies ran while one was open for 11% of the time, Pallas kernels for 0%

commit v1 on v0

v1 whole, which is shorter than its diff:
```python
import functools

import jax
import jax.numpy as jnp
from jax import lax
from jax.experimental import pallas as pl
from jax.experimental.pallas import tpu as pltpu
from jax.sharding import PartitionSpec as P

LANES = 128
SPAN = 512
NEG_PAD = 1024
ROWS = 8192
DUMP = 8192
RELS = 4096
EDGES = 2048
BUCKETS = 32
CHIPS = 4
F32 = jnp.float32
BF16 = jnp.bfloat16
VM = pl.BlockSpec(memory_space=pltpu.VMEM)
SM = pl.BlockSpec(memory_space=pltpu.SMEM)
NT = (((1,), (1,)), ((), ()))
TN = (((0,), (0,)), ((), ()))


def call(kernel, name, outs, ins, scratch=(), flops=1000000, size=4000000):
    return pl.pallas_call(
        kernel,
        name=name,
        out_shape=outs,
        in_specs=ins,
        out_specs=jax.tree.map(lambda _: VM, outs),
        scratch_shapes=scratch,
        compiler_params=pltpu.CompilerParams(vmem_limit_bytes=56 << 20),
        cost_estimate=pl.CostEstimate(flops=flops, bytes_accessed=size, transcendentals=0),
    )


def shape(dims, kind):
    return jax.ShapeDtypeStruct(dims, kind)


def iota(dims, axis):
    return lax.broadcasted_iota(jnp.int32, dims, axis)


def to_column(row):
    size = row.shape[1]
    same = iota((size, size), 0) == iota((size, size), 1)
    return jnp.sum(jnp.where(same, row, 0.0), axis=1, keepdims=True)


def to_row(column):
    size = column.shape[0]
    same = iota((size, size), 0) == iota((size, size), 1)
    return jnp.sum(jnp.where(same, column, 0.0), axis=0, keepdims=True)


def swap_halves(value):
    return pltpu.roll(value, LANES // 2, 1)


def times(left, right):
    lane = iota(left.shape, 1)
    first = lane < LANES // 2
    turned = swap_halves(right)
    real = jnp.where(first, right, turned)
    imag = jnp.where(first, -turned, right)
    return left * real + swap_halves(left) * imag


def times_conj(left, right):
    lane = iota(left.shape, 1)
    first = lane < LANES // 2
    turned = swap_halves(right)
    real = jnp.where(first, right, turned)
    imag = jnp.where(first, turned, -right)
    return left * real + swap_halves(left) * imag


def rank_kernel(owner_ref, row_ref, target_ref, request_ref):
    lower = (iota((LANES, LANES), 0) <= iota((LANES, LANES), 1)).astype(BF16)
    before = jnp.zeros((BUCKETS, 1), F32)
    high = jnp.zeros((BUCKETS, LANES), F32)
    low = jnp.zeros((BUCKETS, LANES), F32)
    for block in range(EDGES // LANES):
        at = slice(block * LANES, (block + 1) * LANES)
        owner = owner_ref[:, at]
        row = row_ref[:, at]
        mine = iota((BUCKETS, LANES), 0) == owner
        hit = mine.astype(F32).astype(BF16)
        count = jnp.dot(hit, lower, preferred_element_type=F32)
        place = jnp.where(mine, count + before - 1.0, 0.0)
        rank = jnp.sum(place, axis=0, keepdims=True)
        before = before + count[:, LANES - 1 : LANES]
        target_ref[:, at] = owner * LANES + rank.astype(jnp.int32)
        slot = iota((LANES, LANES), 0) == rank.astype(jnp.int32)
        upper = jnp.where(slot, (row >> 7).astype(F32), 0.0).astype(BF16)
        under = jnp.where(slot, (row & 127).astype(F32), 0.0).astype(BF16)
        high = high + lax.dot_general(hit, upper, NT, preferred_element_type=F32)
        low = low + lax.dot_general(hit, under, NT, preferred_element_type=F32)
    used = iota((BUCKETS, LANES), 1).astype(F32) < before
    request_ref[...] = jnp.where(used, high * 128.0 + low, float(DUMP)).astype(jnp.int32)


def load_table(table_ref, wide_ref, rows):
    wide_ref[0:rows, :] = table_ref[...].astype(F32)


def gather_kernel(unroll, chip_ref, head_ref, rel_ref, neg_ref, table_ref, rtable_ref,
                  p0, p1, p2, p3, product_ref, heads_ref, rels_ref, negs_ref, wide, rwide):
    load_table(table_ref, wide, ROWS)
    load_table(rtable_ref, rwide, RELS)
    wide[ROWS : ROWS + 8, :] = jnp.zeros((8, LANES), F32)
    for step, pack in enumerate((p0, p1, p2, p3)):
        span = lax.rem(chip_ref[0] + step, CHIPS)

        def edge_step(j, carry):
            base = pl.multiple_of(span * SPAN + j * unroll, unroll)
            head = jnp.concatenate(
                [wide[pl.ds(head_ref[base + r], 1), :] for r in range(unroll)], axis=0)
            rel = jnp.concatenate(
                [rwide[pl.ds(rel_ref[base + r], 1), :] for r in range(unroll)], axis=0)
            product = times(head, rel).astype(BF16)
            at = pl.ds(base, unroll)
            pack[pl.ds(pl.multiple_of(NEG_PAD + j * unroll, unroll), unroll), :] = product
            product_ref[at, :] = product
            heads_ref[at, :] = head.astype(BF16)
            rels_ref[at, :] = rel.astype(BF16)
            return carry

        lax.fori_loop(0, SPAN // unroll, edge_step, 0)

        def neg_step(j, carry):
            base = pl.multiple_of(j * unroll, unroll)
            rows = jnp.concatenate(
                [wide[pl.ds(neg_ref[span, base + r], 1), :] for r in range(unroll)],
                axis=0).astype(BF16)
            pack[pl.ds(base, unroll), :] = rows
            negs_ref[span, pl.ds(base, unroll), :] = rows
            return carry

        lax.fori_loop(0, NEG_PAD // unroll, neg_step, 0)


def found_kernel(unroll, asked_ref, table_ref, found_ref, wide):
    load_table(table_ref, wide, ROWS)
    wide[ROWS : ROWS + 8, :] = jnp.zeros((8, LANES), F32)

    def source(s, carry):
        def group(j):
            base = pl.multiple_of(j * unroll, unroll)
            rows = jnp.concatenate(
                [wide[pl.ds(asked_ref[s, base + r], 1), :] for r in range(unroll)], axis=0)
            found_ref[s, pl.ds(base, unroll), :] = rows.astype(BF16)
            return j + 1

        def more(j):
            first = asked_ref[s, jnp.minimum(j * unroll, LANES - 1)]
            return jnp.logical_and(j * unroll < LANES, first < DUMP)

        lax.while_loop(more, group, 0)
        return carry

    lax.fori_loop(0, BUCKETS, source, 0)


def tail_kernel(unroll, target_ref, fetched_ref, product_ref, tails_ref, partial_ref, slots_ref,
                wide, out_wide, prod_wide):
    wide[...] = fetched_ref[...].astype(F32)
    prod_wide[...] = product_ref[...].astype(F32)
    out_wide[...] = jnp.zeros_like(out_wide)

    def step(j, carry):
        base = pl.multiple_of(j * unroll, unroll)
        rows = []
        for r in range(unroll):
            place = target_ref[0, base + r]
            rows.append(wide[pl.ds(place, 1), :])
            out_wide[pl.ds(place, 1), :] = prod_wide[pl.ds(base + r, 1), :]
        tails_ref[pl.ds(base, unroll), :] = jnp.concatenate(rows, axis=0).astype(BF16)
        return carry

    lax.fori_loop(0, EDGES // unroll, step, 0)
    slots_ref[...] = out_wide[...].astype(BF16)
    for block in range(EDGES // LANES):
        at = slice(block * LANES, (block + 1) * LANES)
        both = tails_ref[at, :].astype(F32) * prod_wide[at, :]
        partial_ref[:, at] = to_row(jnp.sum(both, axis=1, keepdims=True))


def score_kernel(core_ref, q0, q1, q2, q3, keep_ref, send_ref):
    core = core_ref[0]
    parts = (q0, q1, q2, q3)
    for half, out in ((core, keep_ref), (1 - core, send_ref)):
        at = pl.ds(pl.multiple_of(NEG_PAD + half * (SPAN // 2), SPAN // 2), SPAN // 2)
        left = jnp.concatenate([q[at, :] for q in parts], axis=1)
        for piece in range(4):
            cut = slice(piece * 256, (piece + 1) * 256)
            right = jnp.concatenate([q[cut, :] for q in parts], axis=1)
            out[:, cut] = lax.dot_general(left, right, NT, preferred_element_type=F32)


def soft_kernel(negatives, keep_ref, other_ref, weight_ref, stat_ref):
    for block in range(SPAN // 2 // LANES):
        at = slice(block * LANES, (block + 1) * LANES)
        scores = keep_ref[at, :] + other_ref[at, :]
        real = iota((LANES, NEG_PAD), 1) < negatives
        scores = jnp.where(real, scores, -jnp.inf)
        top = jnp.max(scores, axis=1, keepdims=True)
        expo = jnp.exp(scores - top)
        weight_ref[at, :] = expo.astype(BF16)
        stat_ref[0:1, at] = to_row(top)
        stat_ref[1:2, at] = to_row(jnp.sum(expo, axis=1, keepdims=True))


def edge_kernel(unroll, rel_ref, target_ref, positive_ref, stat_ref, weight_ref, negs_ref,
                product_ref, heads_ref, rels_ref, tails_ref,
                loss_ref, head_grad_ref, rel_grad_ref, slot_ref, scaled_ref,
                grad, a0, a1, a2, a3):
    sums = (a0, a1, a2, a3)
    for one in sums:
        one[...] = jnp.zeros_like(one)
    slots = jnp.zeros((BUCKETS, LANES), F32)
    half = SPAN // 2
    for block in range(EDGES // LANES):
        at = slice(block * LANES, (block + 1) * LANES)
        part, inner = block // 2, (block % 2) * LANES
        high = stat_ref[part, 0:1, inner : inner + LANES]
        mass = stat_ref[part, 1:2, inner : inner + LANES]
        positive = positive_ref[:, at]
        top = jnp.maximum(high, positive)
        shrink = jnp.exp(high - top)
        expo = jnp.exp(positive - top)
        total = mass * shrink + expo
        scale = shrink / total
        slope = expo / total - 1.0
        loss_ref[:, at] = top + jnp.log(total) - positive
        target = target_ref[:, at]
        hit = (iota((BUCKETS, LANES), 0) == (target >> 7)).astype(F32).astype(BF16)
        slot = iota((LANES, LANES), 0) == (target & 127)
        rest = slope
        for _ in range(3):
            piece = rest.astype(BF16)
            spread = jnp.where(slot, piece.astype(F32), 0.0).astype(BF16)
            slots = slots + lax.dot_general(hit, spread, NT, preferred_element_type=F32)
            rest = rest - piece.astype(F32)
        scale_col = to_column(scale)
        slope_col = to_column(slope)
        scaled_ref[at, :] = (product_ref[at, :].astype(F32) * scale_col).astype(BF16)
        raw = jnp.dot(weight_ref[at, :], negs_ref[block // 4], preferred_element_type=F32)
        down = raw * scale_col + slope_col * tails_ref[at, :].astype(F32)
        head_grad_ref[at, :] = times_conj(down, rels_ref[at, :].astype(F32))
        grad[at, :] = times_conj(down, heads_ref[at, :].astype(F32))
    slot_ref[...] = slots

    def step(j, carry):
        for r in range(unroll):
            for k, one in enumerate(sums):
                edge = k * SPAN + j * unroll + r
                place = pl.ds(rel_ref[edge], 1)
                one[place, :] = one[place, :] + grad[pl.ds(edge, 1), :]
        return carry

    lax.fori_loop(0, SPAN // unroll, step, 0)
    rel_grad_ref[...] = ((a0[...] + a1[...]) + (a2[...] + a3[...])).astype(BF16)


def entity_kernel(unroll, negatives, head_ref, neg_ref, weight_ref, scaled_ref, head_grad_ref,
                  out_ref, grad, a0, a1, a2, a3):
    sums = (a0, a1, a2, a3)
    for one in sums:
        one[...] = jnp.zeros_like(one)
    for span in range(CHIPS):
        at = slice(span * SPAN, (span + 1) * SPAN)
        grad[span] = lax.dot_general(
            weight_ref[at, :], scaled_ref[at, :], TN, preferred_element_type=F32)

    def edge_step(j, carry):
        for r in range(unroll):
            for k, one in enumerate(sums):
                edge = k * SPAN + j * unroll + r
                place = pl.ds(head_ref[edge], 1)
                one[place, :] = one[place, :] + head_grad_ref[pl.ds(edge, 1), :]
        return carry

    lax.fori_loop(0, SPAN // unroll, edge_step, 0)

    def neg_step(j, carry):
        for r in range(unroll):
            for k, one in enumerate(sums):
                place = pl.ds(neg_ref[k, j * unroll + r], 1)
                one[place, :] = one[place, :] + grad[k, pl.ds(j * unroll + r, 1), :]
        return carry

    lax.fori_loop(0, negatives // unroll, neg_step, 0)
    total = (a0[0:ROWS, :] + a1[0:ROWS, :]) + (a2[0:ROWS, :] + a3[0:ROWS, :])
    out_ref[...] = total


def owner_kernel(unroll, asked_ref, slope_ref, came_ref, part_ref, out_ref,
                 wide, a0, a1, a2, a3):
    sums = (a0, a1, a2, a3)
    for one in sums[1:]:
        one[...] = jnp.zeros_like(one)
    a0[0:ROWS, :] = part_ref[...]
    a0[ROWS : ROWS + 8, :] = jnp.zeros((8, LANES), F32)
    wide[...] = came_ref[...].astype(F32)
    each = BUCKETS // 4

    def source(s, carry):
        def group(j):
            for r in range(unroll):
                for k, one in enumerate(sums):
                    owner = k * each + s
                    slot = j * unroll + r
                    place = pl.ds(asked_ref[owner, slot], 1)
                    term = slope_ref[owner, slot] * wide[pl.ds(owner * LANES + slot, 1), :]
                    one[place, :] = one[place, :] + term
            return j + 1

        def more(j):
            at = jnp.minimum(j * unroll, LANES - 1)
            first = asked_ref[s, at]
            for k in range(1, 4):
                first = jnp.minimum(first, asked_ref[k * each + s, at])
            return jnp.logical_and(j * unroll < LANES, first < DUMP)

        lax.while_loop(more, group, 0)
        return carry

    lax.fori_loop(0, each, source, 0)
    total = (a0[0:ROWS, :] + a1[0:ROWS, :]) + (a2[0:ROWS, :] + a3[0:ROWS, :])
    out_ref[...] = total


def body(entity_table, relation_table, head_row, relation_id, tail_owner, tail_row, negative_row):
    negatives = negative_row.shape[1]
    place = lax.axis_index("col")
    chip = (place // 2).astype(jnp.int32).reshape(1)
    core = (place % 2).astype(jnp.int32).reshape(1)
    pad = jnp.pad(negative_row, ((0, 0), (0, NEG_PAD - negatives)), constant_values=DUMP)
    pack = shape((NEG_PAD + SPAN, LANES), BF16)
    flat = shape((EDGES, LANES), BF16)
    wide = pltpu.VMEM((ROWS + 8, LANES), F32)

    target, request = call(
        rank_kernel, "rank",
        (shape((1, EDGES), jnp.int32), shape((BUCKETS, LANES), jnp.int32)), [VM, VM],
    )(tail_owner.reshape(1, EDGES), tail_row.reshape(1, EDGES))
    asked = lax.all_to_all(request, "bucket", split_axis=0, concat_axis=0, tiled=True)

    p0, p1, p2, p3, product, heads, rels, negs = call(
        functools.partial(gather_kernel, 32), "gather",
        (pack, pack, pack, pack, flat, flat, flat, shape((CHIPS, NEG_PAD, LANES), BF16)),
        [SM, SM, SM, SM, VM, VM],
        [wide, pltpu.VMEM((RELS, LANES), F32)], size=30000000,
    )(chip, head_row, relation_id, pad, entity_table, relation_table)

    def along(step):
        return [(2 * x + c, 2 * ((x + step) % CHIPS) + c) for x in range(CHIPS) for c in range(2)]

    q1 = lax.ppermute(p1, "col", along(1))
    q2 = lax.ppermute(p2, "col", along(2))
    q3 = lax.ppermute(p3, "col", along(3))

    found = call(
        functools.partial(found_kernel, 32), "found",
        shape((BUCKETS, LANES, LANES), BF16), [SM, VM], [wide], size=15000000,
    )(asked, entity_table)
    fetched = lax.all_to_all(found, "bucket", split_axis=0, concat_axis=0, tiled=True)

    half = shape((SPAN // 2, NEG_PAD), F32)
    keep, send = call(score_kernel, "scores", (half, half), [SM, VM, VM, VM, VM],
                      flops=500000000)(core, p0, q1, q2, q3)
    other = lax.ppermute(send, "col", [(c, c ^ 1) for c in range(8)])
    weight, stat = call(
        functools.partial(soft_kernel, negatives), "soft",
        (shape((SPAN // 2, NEG_PAD), BF16), shape((2, SPAN // 2), F32)), [VM, VM],
    )(keep, other)
    weights = lax.all_gather(weight, "col", axis=0, tiled=True)
    stats = lax.all_gather(stat, "col", axis=0)

    tails, partial, slots = call(
        functools.partial(tail_kernel, 32), "tails",
        (flat, shape((1, EDGES), F32), shape((BUCKETS * LANES, LANES), BF16)), [SM, VM, VM],
        [pltpu.VMEM((BUCKETS * LANES, LANES), F32), pltpu.VMEM((BUCKETS * LANES, LANES), F32),
         pltpu.VMEM((EDGES, LANES), F32)], size=15000000,
    )(target, fetched.reshape(BUCKETS * LANES, LANES), product)
    positive = lax.psum(partial, "col")
    came = lax.all_to_all(slots.reshape(BUCKETS, LANES, LANES), "bucket",
                          split_axis=0, concat_axis=0, tiled=True)

    loss, head_grad, rel_local, slope, scaled = call(
        functools.partial(edge_kernel, 8), "edges",
        (shape((1, EDGES), F32), shape((EDGES, LANES), F32), shape((RELS, LANES), BF16),
         shape((BUCKETS, LANES), F32), flat),
        [SM] + [VM] * 9,
        [pltpu.VMEM((EDGES, LANES), F32)] + [pltpu.VMEM((RELS, LANES), F32)] * 4,
        size=20000000,
    )(relation_id, target, positive, stats, weights, negs, product, heads, rels, tails)
    slopes = lax.all_to_all(slope, "bucket", split_axis=0, concat_axis=0, tiled=True)
    rel_parts = lax.all_to_all(rel_local.reshape(BUCKETS, LANES, LANES), "bucket",
                               split_axis=0, concat_axis=0, tiled=True)

    part = call(
        functools.partial(entity_kernel, 8, negatives), "entities", shape((ROWS, LANES), F32),
        [SM, SM, VM, VM, VM],
        [pltpu.VMEM((CHIPS, NEG_PAD, LANES), F32)] + [wide] * 4, size=40000000,
    )(head_row, pad, weights, scaled, head_grad)
    grad = call(
        functools.partial(owner_kernel, 8), "owners", shape((ROWS, LANES), F32),
        [SM, SM, VM, VM],
        [pltpu.VMEM((BUCKETS * LANES, LANES), F32)] + [wide] * 4, size=30000000,
    )(asked, slopes, came.reshape(BUCKETS * LANES, LANES), part)
    relation_grad = jnp.sum(rel_parts.astype(F32), axis=0)
    return (loss.reshape(EDGES), grad, relation_grad)


def solution(mesh):
    in_specs = (
        P("bucket", "col"),
        P(None, "col"),
        P("bucket"),
        P("bucket"),
        P("bucket", None),
        P("bucket"),
        P("bucket", None),
    )
    out_specs = (P("bucket"), P("bucket", "col"), P("bucket", "col"))
    return jax.shard_map(body, mesh=mesh, in_specs=in_specs, out_specs=out_specs, check_vma=False)
```

time: 791 us -> 247 us (0.31)
  waiting for transfers between devices: 445 us -> 18.9 us
  other arithmetic: 135 us -> 0.78 us
  local copies, waits for them, and re-layouts: 122 us -> 3.18 us
  Pallas kernels: 0 us -> 87 us
  blocking collectives: 32.9 us -> 103 us
  matrix products: 21.1 us -> 0 us
    psum x4 -> x0, waiting for transfers between devices: 280 us -> none  [span_step(): scores = lax.psum(partial_value, 'col')]
    reduce_scatter x1 -> x0, waiting for transfers between devices: 131 us -> none  [body(): lax.psum_scatter(rel_local, 'bucket', scatter_dimension=0, tiled=True)]
    scatter-add x7 -> x0, other arithmetic: 93.3 us -> none  [the longest x4 40.7 us: span_step(): grad = grad.at[negs].add(neg_grad)]
    pallas_call x0 -> x9, Pallas kernels: none -> 87 us  [the longest x1 23.2 us: body(): call(functools.partial(gather_kernel, 32), 'gather', (pack, pack, pack, p...]
    all_to_all x0 -> x2, blocking collectives: none -> 54.9 us  [the longest x1 36.6 us: body(): lax.all_to_all(found, 'bucket', split_axis=0, concat_axis=0, tiled=True)]
    gather x8 -> x0, local copies, waits for them, and re-layouts: 53.4 us -> none  [the longest x1 14.9 us: body(): found = entity_table[asked]]
    all_to_all x2, waiting for transfers between devices: 34 us -> 0.01 us  [the longest x1 0.01 us: body(): lax.all_to_all(rel_local.reshape(BUCKETS, LANES, LANES), 'bucket', split_...]
    dynamic_update_slice x16 -> x0, local copies, waits for them, and re-layouts: 25.4 us -> none  [body(): grad, (loss, prod_grad, pos_grad) = lax.scan(span_step, start, inputs)]
  transfers between devices with their start and end apart: 7 -> 7, of which waited for: 6 -> 3; matrix products, arithmetic and copies ran while one was open for 11% -> 0% of each run, Pallas kernels for 0% -> 24%
where the time goes in v1:
time: 247 us; the launch traced here: 243 us
  blocking collectives  103 us (42%)
  Pallas kernels  87 us (35%)
  waiting for transfers between devices  18.9 us (8%)
  starting transfers between devices  15.8 us (6%)
  between operations  14.1 us (6%)
  local copies, waits for them, and re-layouts  3.18 us (1%)
    all_to_all x1, blocking collectives, body(): lax.all_to_all(found, 'bucket', split_axis=0, concat_axis=0, tiled=True)  36.6 us
    pallas_call x1, Pallas kernels, body(): call(functools.partial(gather_kernel, 32), 'gather', (pack, pack, pack, p...  23.2 us
    all_to_all x1, blocking collectives, body(): lax.all_to_all(request, 'bucket', split_axis=0, concat_axis=0, tiled=True)  20 us
    all_to_all x1, blocking collectives, body(): lax.all_to_all(slope, 'bucket', split_axis=0, concat_axis=0, tiled=True)  18.4 us
    pallas_call x1, Pallas kernels, body(): call(functools.partial(entity_kernel, 8, negatives), 'entities', shape((R...  16.5 us
    psum x1, blocking collectives, body(): positive = lax.psum(partial, 'col')  15.5 us
    all_gather x1, blocking collectives, body(): stats = lax.all_gather(stat, 'col', axis=0)  12.4 us
    pallas_call x1, Pallas kernels, body(): call(functools.partial(owner_kernel, 8), 'owners', shape((ROWS, LANES), F...  12.1 us
  transfers between devices with their start and end apart: 7, of which 3 were waited for; matrix products, arithmetic and copies ran while one was open for 0% of the time, Pallas kernels for 24%

profile of v1, /device:TPU:32, one launch (start us, length us, event | category | flops | bytes accessed | tf_op | source)
XLA Modules:
  0.0 242.6 jit_solution(10624915499017345907)
XLA Ops:
  7.2 0.0 all-gather.4.cloned.1.call-start
  7.2 1.3 pad.4.neg_ref
  8.5 23.2 %gather.1 = (bf16[1536,128]{1,0:T(8,128)(2,1)}, bf16[1536,128]{1,0:T(8,128)(2,1)}, bf16[1536,128]{1,0:T(8,128)(2,1)}, bf16[1536,128]{1,0:T(8,128)(2,1)}, bf16[20...) custom-call(s32[1]{0:T(128)} %bitcast.6.chip_ref, ...), custom_call_target="tpu_custom_call" | custom-call | flops 1000000 | bytes 30000000 | tf_op jit(solution)/shard_map/gather/pallas_call | solution.py:354
  31.8 1.5 collective-permute-start
  33.3 2.7 %collective-permute-start.1 = (bf16[1536,128]{1,0:T(8,128)(2,1)}, bf16[1536,128]{1,0:T(8,128)(2,1)S(1)}, u32[]{:S(2)}, u32[]{:S(2)}) collective-permute-start(bf16[1536,128]{1,0:T(8,128)(2,1)} %get-tuple-element.31), channel_id=1, source_target_pairs={{0,4},{1,5},{2,6},{3,7},{4,0},{5,1},{6,2},{7,3},{8,12},{9,13},{10,... | collective-permute-start | bytes 1179656 | tf_op jit(solution)/shard_map/ppermute | solution.py:365
  36.0 1.4 collective-permute-start.2
  37.4 6.8 %collective-permute-done.q1 = bf16[1536,128]{1,0:T(8,128)(2,1)S(1)} collective-permute-done((bf16[1536,128]{1,0:T(8,128)(2,1)}, bf16[1536,128]{1,0:T(8,128)(2,1)S(1)}, u32[]{:S(2)}, u32[]{:S(2)}) %collective-permute-start) | collective-permute-done | bytes 393248 | tf_op jit(solution)/shard_map/ppermute | solution.py:364
  44.2 0.0 copy-start.3
  44.2 9.2 %collective-permute-done.1.q2 = bf16[1536,128]{1,0:T(8,128)(2,1)S(1)} collective-permute-done((bf16[1536,128]{1,0:T(8,128)(2,1)}, bf16[1536,128]{1,0:T(8,128)(2,1)S(1)}, u32[]{:S(2)}, u32[]{:S(2)}) %collective-permute-start.1) | collective-permute-done | bytes 393248 | tf_op jit(solution)/shard_map/ppermute | solution.py:365
  53.4 0.0 copy-start.4
  53.5 0.0 collective-permute-done.2.q3
  53.5 0.0 copy-start.5
  53.5 0.0 copy-done.3
  53.5 0.7 copy-done.4
  54.2 0.1 copy-done.5
  54.3 3.2 %scores.1 = (f32[256,1024]{1,0:T(8,128)}, f32[256,1024]{1,0:T(8,128)}) custom-call(s32[1]{0:T(128)} %bitcast.7.core_ref, bf16[1536,128]{1,0:T(8,128)(2,1)} %get-tuple-element.29.q0, bf16[1536,128]{1,0:T(8,128)(2,1)} %copy-done.3, bf16[1536,128]{1,0:T(8,128)(2,1)} %copy-done.4, bf16[1536,128]{1,0:T(8,128)(2,1)} %copy-done.5), custom_call_target="tpu_custom_call" | custom-call | flops 500000000 | bytes 4000000 | tf_op jit(solution)/shard_map/scores/pallas_call | solution.py:375
  57.5 0.0 collective-permute-start.3
  57.5 2.9 %collective-permute-done.3.other_ref = f32[256,1024]{1,0:T(8,128)S(1)} collective-permute-done((f32[256,1024]{1,0:T(8,128)}, f32[256,1024]{1,0:T(8,128)S(1)}, u32[]{:S(2)}, u32[]{:S(2)}) %collective-permute-start.3) | collective-permute-done | bytes 1048608 | tf_op jit(solution)/shard_map/ppermute | solution.py:377
  60.3 0.0 copy-start.1
  60.3 1.0 copy-done.1
  61.3 2.6 %soft.1 = (bf16[256,1024]{1,0:T(8,128)(2,1)}, f32[2,256]{1,0:T(2,128)}) custom-call(f32[256,1024]{1,0:T(8,128)} %get-tuple-element.33.keep_ref, f32[256,1024]{1,0:T(8,128)} %copy-done.1), custom_call_target="tpu_custom_call" | custom-call | flops 1000000 | bytes 4000000 | tf_op jit(solution)/shard_map/soft/pallas_call | solution.py:378
  64.0 0.0 all-gather.4.cloned.1.call-update
  64.0 4.3 %rank.1 = (s32[1,2048]{1,0:T(1,128)}, s32[32,128]{1,0:T(8,128)}) custom-call(s32[1,2048]{1,0:T(1,128)} %bitcast.27, s32[1,2048]{1,0:T(1,128)} %bitcast.28), custom_call_target="tpu_custom_call" | custom-call | flops 1000000 | bytes 4000000 | tf_op jit(solution)/shard_map/rank/pallas_call | solution.py:348
  68.3 20.0 %all_to_all.37 = s32[32,1,128]{2,1,0:T(1,128)} all-to-all(s32[32,1,128]{2,1,0:T(1,128)} %bitcast.26), channel_id=1, replica_groups=mesh['bucket'=32,'col'=8] {'bucket'}, dimensions={0} | all-to-all | bytes 32768 | tf_op jit(solution)/shard_map/all_to_all | solution.py:352
  88.3 0.0 copy-start.2
  88.3 8.6 %found.1 = bf16[32,128,128]{2,1,0:T(8,128)(2,1)} custom-call(s32[32,128]{1,0:T(8,128)} %bitcast.22, bf16[8192,128]{1,0:T(8,128)(2,1)} %table_ref.3), custom_call_target="tpu_custom_call" | custom-call | flops 1000000 | bytes 15000000 | tf_op jit(solution)/shard_map/found/pallas_call | solution.py:368
  96.9 36.6 %all_to_all.38 = bf16[32,128,128]{2,1,0:T(8,128)(2,1)} all-to-all(bf16[32,128,128]{2,1,0:T(8,128)(2,1)} %found.1), channel_id=1, replica_groups=mesh['bucket'=32,'col'=8] {'bucket'}, dimensions={0} | all-to-all | bytes 2097152 | tf_op jit(solution)/shard_map/all_to_all | solution.py:372
  133.4 6.1 %tails.1 = (bf16[2048,128]{1,0:T(8,128)(2,1)}, f32[1,2048]{1,0:T(1,128)}, bf16[4096,128]{1,0:T(8,128)(2,1)}) custom-call(s32[1,2048]{1,0:T(1,128)} %get-tuple-element.25.target_ref, bf16[4096,128]{1,0:T(8,128)(2,1)} %bitcast.19, bf16[2048,128]{1,0:T(8,128)(2,1)} %get-tuple-element.27.product_ref), custom_call_target="tpu_custom_call" | custom-call | flops 1000000 | bytes 15000000 | tf_op jit(solution)/shard_map/tails/pallas_call | solution.py:385
  139.5 5.1 %all-to-all-start.3 = ((bf16[32,128,128]{2,1,0:T(8,128)(2,1)}), bf16[32,128,128]{2,1,0:T(8,128)(2,1)S(1)}, u32[]{:S(2)}, u32[]{:S(2)}) async-start(bf16[32,128,128]{2,1,0:T(8,128)(2,1)} %bitcast.21), calls=%async_computation.3 | async-start | bytes 2097152 | tf_op jit(solution)/shard_map/all_to_all | solution.py:392
  144.6 0.0 copy-done.2
  144.7 12.4 %all-gather.1.stat_ref = f32[8,2,256]{2,1,0:T(2,128)} all-gather(f32[1,2,256]{2,1,0:T(2,128)S(1)} %bitcast.29), channel_id=2, replica_groups=mesh['bucket'=32,'col'=8] {'col'}, dimensions={0}, use_global_device_ids=true | all-gather | bytes 18432 | tf_op jit(solution)/shard_map/all_gather | solution.py:383
  157.0 15.5 %psum.7.positive_ref = f32[1,2048]{1,0:T(1,128)} all-reduce(f32[1,2048]{1,0:T(1,128)} %get-tuple-element.28), channel_id=1, replica_groups=mesh['bucket'=32,'col'=8] {'col'}, use_global_device_ids=true, to_apply=%region_0.1 | all-reduce | flops 2048 | bytes 16384 | tf_op jit(solution)/shard_map/psum | solution.py:391
  172.5 0.0 all-gather.4.cloned.1.call-done.weight_ref
  172.5 10.5 %edges.1 = (f32[1,2048]{1,0:T(1,128)}, f32[2048,128]{1,0:T(8,128)}, bf16[4096,128]{1,0:T(8,128)(2,1)}, f32[32,128]{1,0:T(8,128)}, bf16[2048,128]{1,0:T(8,128)(2,1)}) custom-call(s32[2048]{0:T(1024)} %rel_ref.3, s32[1,2048]{1,0:T(1,128)} %get-tuple-element.25.target_ref, f32[1,2048]{1,0:T(1,128)} %psum.7.positive_ref, f32[8,2,256]{2,1,0:T(2,128)} %all-gather.1.stat_ref, ...), custom_call_target="tpu_custom_call" | custom-call | flops 1000000 | bytes 20000000 | tf_op jit(solution)/shard_map/edges/pallas_call | solution.py:395
  183.0 0.0 all-to-all-done.3
  183.0 0.0 copy-start
  183.0 18.4 %all_to_all.39 = f32[32,1,128]{2,1,0:T(1,128)} all-to-all(f32[32,1,128]{2,1,0:T(1,128)} %bitcast.25), channel_id=1, replica_groups=mesh['bucket'=32,'col'=8] {'bucket'}, dimensions={0} | all-to-all | bytes 32768 | tf_op jit(solution)/shard_map/all_to_all | solution.py:403
  201.3 5.0 %all-to-all-start.4 = ((bf16[32,128,128]{2,1,0:T(8,128)(2,1)}), bf16[32,128,128]{2,1,0:T(8,128)(2,1)S(1)}, u32[]{:S(2)}, u32[]{:S(2)}) async-start(bf16[32,128,128]{2,1,0:T(8,128)(2,1)} %bitcast.20), calls=%async_computation.4 | async-start | bytes 2097152 | tf_op jit(solution)/shard_map/all_to_all | solution.py:404
  206.3 16.5 %entities.1.part_ref = f32[8192,128]{1,0:T(8,128)} custom-call(s32[2048]{0:T(1024)} %head_ref.3, s32[4,1024]{1,0:T(4,128)} %pad.4.neg_ref, bf16[2048,1024]{1,0:T(8,128)(2,1)} %all-gather.4.cloned.1.call-done.weight_ref, bf16[2048,128]{1,0:T(8,128)(2,1)} %get-tuple-element.44.scaled_ref, f32[2048,128]{1,0:T(8,128)} %get-tuple-element.45.head_grad_ref), custom_call_target="tpu_custom_call" | custom-call | flops 1000000 | bytes 40000000 | tf_op jit(solution)/shard_map/entities/pallas_call | solution.py:407
  222.8 0.0 copy-done
  222.8 12.1 %owners.1 = f32[8192,128]{1,0:T(8,128)} custom-call(s32[32,128]{1,0:T(8,128)} %bitcast.23, f32[32,128]{1,0:T(8,128)} %bitcast.24, bf16[4096,128]{1,0:T(8,128)(2,1)} %bitcast.18, f32[8192,128]{1,0:T(8,128)} %entities.1.part_ref), custom_call_target="tpu_custom_call" | custom-call | flops 1000000 | bytes 30000000 | tf_op jit(solution)/shard_map/owners/pallas_call | solution.py:412
  234.9 0.0 all-to-all-done.4
  234.9 0.8 convert_reduce_fusion
Async XLA Ops:
  7.2 165.3 %all-gather.4.cloned.1.call-start = ((), (), s32[]{:S(2)}) async-start(), calls=%async_computation.5 | async-start | bytes 4718592 | tf_op jit(solution)/shard_map/all_gather | solution.py:382
  31.8 12.4 %collective-permute-start = (bf16[1536,128]{1,0:T(8,128)(2,1)}, bf16[1536,128]{1,0:T(8,128)(2,1)S(1)}, u32[]{:S(2)}, u32[]{:S(2)}) collective-permute-start(bf16[1536,128]{1,0:T(8,128)(2,1)} %get-tuple-element.30), channel_id=1, source_target_pairs={{0,2},{1,3},{2,4},{3,5},{4,6},{5,7},{6,0},{7,1},{8,10},{9,11},{10,... | collective-permute-start | bytes 1179656 | tf_op jit(solution)/shard_map/ppermute | solution.py:364
  33.3 20.2 %collective-permute-start.1 = (bf16[1536,128]{1,0:T(8,128)(2,1)}, bf16[1536,128]{1,0:T(8,128)(2,1)S(1)}, u32[]{:S(2)}, u32[]{:S(2)}) collective-permute-start(bf16[1536,128]{1,0:T(8,128)(2,1)} %get-tuple-element.31), channel_id=1, source_target_pairs={{0,4},{1,5},{2,6},{3,7},{4,0},{5,1},{6,2},{7,3},{8,12},{9,13},{10,... | collective-permute-start | bytes 1179656 | tf_op jit(solution)/shard_map/ppermute | solution.py:365
  36.0 17.5 %collective-permute-start.2 = (bf16[1536,128]{1,0:T(8,128)(2,1)}, bf16[1536,128]{1,0:T(8,128)(2,1)S(1)}, u32[]{:S(2)}, u32[]{:S(2)}) collective-permute-start(bf16[1536,128]{1,0:T(8,128)(2,1)} %get-tuple-element.32), channel_id=1, source_target_pairs={{0,6},{1,7},{2,0},{3,1},{4,2},{5,3},{6,4},{7,5},{8,14},{9,15},{10,... | collective-permute-start | bytes 1179656 | tf_op jit(solution)/shard_map/ppermute | solution.py:366
  44.2 9.3 %copy-start.3 = (bf16[1536,128]{1,0:T(8,128)(2,1)}, bf16[1536,128]{1,0:T(8,128)(2,1)S(1)}, u32[]{:S(2)}) copy-start(bf16[1536,128]{1,0:T(8,128)(2,1)S(1)} %collective-permute-done.q1) | copy-start | bytes 1179652
  53.4 0.7 copy-start.4
  53.5 0.9 copy-start.5
  57.5 2.9 %collective-permute-start.3 = (f32[256,1024]{1,0:T(8,128)}, f32[256,1024]{1,0:T(8,128)S(1)}, u32[]{:S(2)}, u32[]{:S(2)}) collective-permute-start(f32[256,1024]{1,0:T(8,128)} %get-tuple-element.34), channel_id=1, source_target_pairs={{0,1},{1,0},{2,3},{3,2},{4,5},{5,4},{6,7},{7,6},{8,9},{9,8},{10,11... | collective-permute-start | bytes 3145736 | tf_op jit(solution)/shard_map/ppermute | solution.py:377
  60.3 1.0 copy-start.1
  88.3 56.4 %copy-start.2 = (f32[2,256]{1,0:T(2,128)S(1)}, f32[2,256]{1,0:T(2,128)}, u32[]{:S(2)}) copy-start(f32[2,256]{1,0:T(2,128)} %get-tuple-element.35) | copy-start | bytes 6148
  139.5 43.5 %all-to-all-start.3 = ((bf16[32,128,128]{2,1,0:T(8,128)(2,1)}), bf16[32,128,128]{2,1,0:T(8,128)(2,1)S(1)}, u32[]{:S(2)}, u32[]{:S(2)}) async-start(bf16[32,128,128]{2,1,0:T(8,128)(2,1)} %bitcast.21), calls=%async_computation.3 | async-start | bytes 2097152 | tf_op jit(solution)/shard_map/all_to_all | solution.py:392
  183.0 39.9 %copy-start = (bf16[32,128,128]{2,1,0:T(8,128)(2,1)}, bf16[32,128,128]{2,1,0:T(8,128)(2,1)S(1)}, u32[]{:S(2)}) copy-start(bf16[32,128,128]{2,1,0:T(8,128)(2,1)S(1)} %all-to-all-done.3) | copy-start | bytes 3145732
  201.3 33.6 %all-to-all-start.4 = ((bf16[32,128,128]{2,1,0:T(8,128)(2,1)}), bf16[32,128,128]{2,1,0:T(8,128)(2,1)S(1)}, u32[]{:S(2)}, u32[]{:S(2)}) async-start(bf16[32,128,128]{2,1,0:T(8,128)(2,1)} %bitcast.20), calls=%async_computation.4 | async-start | bytes 2097152 | tf_op jit(solution)/shard_map/all_to_all | solution.py:404
Sparse Core Ops, SparseCore 0:
  64.1 36.7 all-gather.3

commit v2 on v1

--- a/solution.py
+++ b/solution.py
@@ -24,7 +24,8 @@
 TN = (((0,), (0,)), ((), ()))
 
 
-def call(kernel, name, outs, ins, scratch=(), flops=1000000, size=4000000):
+def call(kernel, name, outs, ins, scratch=(), flops=1000000, size=4000000, group=None):
+    remote = {} if group is None else dict(collective_id=group, has_side_effects=True)
     return pl.pallas_call(
         kernel,
         name=name,
@@ -32,7 +33,7 @@
         in_specs=ins,
         out_specs=jax.tree.map(lambda _: VM, outs),
         scratch_shapes=scratch,
-        compiler_params=pltpu.CompilerParams(vmem_limit_bytes=56 << 20),
+        compiler_params=pltpu.CompilerParams(vmem_limit_bytes=56 << 20, **remote),
         cost_estimate=pl.CostEstimate(flops=flops, bytes_accessed=size, transcendentals=0),
     )
 
@@ -79,7 +80,81 @@
     return left * real + swap_halves(left) * imag
 
 
-def rank_kernel(owner_ref, row_ref, target_ref, request_ref):
+def greet(axis, count):
+    me = lax.axis_index(axis)
+    barrier = pltpu.get_barrier_semaphore()
+
+    def tell(i, carry):
+        peer = lax.rem(me + i, count)
+        pl.semaphore_signal(barrier, inc=1, device_id={axis: peer},
+                            device_id_type=pl.DeviceIdType.MESH)
+        return carry
+
+    lax.fori_loop(1, count, tell, 0)
+    pl.semaphore_wait(barrier, count - 1)
+
+
+def spread(axis, count, src, dst, send_sem, recv_sem):
+    me = lax.axis_index(axis)
+
+    def send(i, carry):
+        peer = lax.rem(me + i, count)
+        pltpu.make_async_remote_copy(
+            src_ref=src.at[peer], dst_ref=dst.at[me], send_sem=send_sem, recv_sem=recv_sem,
+            device_id={axis: peer}, device_id_type=pl.DeviceIdType.MESH).start()
+        return carry
+
+    lax.fori_loop(1, count, send, 0)
+
+
+def settle(axis, count, src, dst, send_sem, recv_sem):
+    me = lax.axis_index(axis)
+    rest = pl.ds(0, count - 1)
+    pltpu.make_async_remote_copy(
+        src_ref=src.at[rest], dst_ref=dst.at[rest], send_sem=send_sem, recv_sem=recv_sem,
+        device_id={axis: lax.rem(me + 1, count)}, device_id_type=pl.DeviceIdType.MESH).wait()
+
+
+def slope_kernel(slope_ref, out_ref, send_sem, recv_sem):
+    greet("bucket", BUCKETS)
+    spread("bucket", BUCKETS, slope_ref, out_ref, send_sem, recv_sem)
+    me = lax.axis_index("bucket")
+    out_ref[me] = slope_ref[me]
+    settle("bucket", BUCKETS, slope_ref, out_ref, send_sem, recv_sem)
+
+
+def share_kernel(cols, partial_ref, stat_ref, positive_ref, stats_ref, parts,
+                 send_sem, recv_sem):
+    greet("col", cols)
+    me = lax.axis_index("col")
+    kept = (partial_ref, stat_ref)
+    lands = (parts, stats_ref)
+
+    def send(i, carry):
+        peer = lax.rem(me + i, cols)
+        for k in range(2):
+            pltpu.make_async_remote_copy(
+                src_ref=kept[k], dst_ref=lands[k].at[me], send_sem=send_sem.at[k],
+                recv_sem=recv_sem.at[k], device_id={"col": peer},
+                device_id_type=pl.DeviceIdType.MESH).start()
+        return carry
+
+    lax.fori_loop(1, cols, send, 0)
+    parts[me] = partial_ref[...]
+    stats_ref[me] = stat_ref[...]
+    rest = pl.ds(0, cols - 1)
+    for k in range(2):
+        pltpu.make_async_remote_copy(
+            src_ref=lands[k].at[rest], dst_ref=lands[k].at[rest], send_sem=send_sem.at[k],
+            recv_sem=recv_sem.at[k], device_id={"col": lax.rem(me + 1, cols)},
+            device_id_type=pl.DeviceIdType.MESH).wait()
+    total = parts[0]
+    for k in range(1, cols):
+        total = total + parts[k]
+    positive_ref[...] = total
+
+
+def rank_kernel(owner_ref, row_ref, target_ref, asked_ref, request_ref, send_sem, recv_sem):
     lower = (iota((LANES, LANES), 0) <= iota((LANES, LANES), 1)).astype(BF16)
     before = jnp.zeros((BUCKETS, 1), F32)
     high = jnp.zeros((BUCKETS, LANES), F32)
@@ -101,7 +176,14 @@
         high = high + lax.dot_general(hit, upper, NT, preferred_element_type=F32)
         low = low + lax.dot_general(hit, under, NT, preferred_element_type=F32)
     used = iota((BUCKETS, LANES), 1).astype(F32) < before
-    request_ref[...] = jnp.where(used, high * 128.0 + low, float(DUMP)).astype(jnp.int32)
+    request = jnp.where(used, high * 128.0 + low, float(DUMP)).astype(jnp.int32)
+    for owner in range(BUCKETS):
+        request_ref[owner] = request[owner : owner + 1, :]
+    greet("bucket", BUCKETS)
+    spread("bucket", BUCKETS, request_ref, asked_ref, send_sem, recv_sem)
+    me = lax.axis_index("bucket")
+    asked_ref[me] = request_ref[me]
+    settle("bucket", BUCKETS, request_ref, asked_ref, send_sem, recv_sem)
 
 
 def load_table(table_ref, wide_ref, rows):
@@ -135,7 +217,7 @@
         def neg_step(j, carry):
             base = pl.multiple_of(j * unroll, unroll)
             rows = jnp.concatenate(
-                [wide[pl.ds(neg_ref[span, base + r], 1), :] for r in range(unroll)],
+                [wide[pl.ds(neg_ref[span * NEG_PAD + j * unroll + r], 1), :] for r in range(unroll)],
                 axis=0).astype(BF16)
             pack[pl.ds(base, unroll), :] = rows
             negs_ref[span, pl.ds(base, unroll), :] = rows
@@ -152,12 +234,12 @@
         def group(j):
             base = pl.multiple_of(j * unroll, unroll)
             rows = jnp.concatenate(
-                [wide[pl.ds(asked_ref[s, base + r], 1), :] for r in range(unroll)], axis=0)
+                [wide[pl.ds(asked_ref[s * LANES + j * unroll + r], 1), :] for r in range(unroll)], axis=0)
             found_ref[s, pl.ds(base, unroll), :] = rows.astype(BF16)
             return j + 1
 
         def more(j):
-            first = asked_ref[s, jnp.minimum(j * unroll, LANES - 1)]
+            first = asked_ref[s * LANES + jnp.minimum(j * unroll, LANES - 1)]
             return jnp.logical_and(j * unroll < LANES, first < DUMP)
 
         lax.while_loop(more, group, 0)
@@ -176,7 +258,7 @@
         base = pl.multiple_of(j * unroll, unroll)
         rows = []
         for r in range(unroll):
-            place = target_ref[0, base + r]
+            place = target_ref[base + r]
             rows.append(wide[pl.ds(place, 1), :])
             out_wide[pl.ds(place, 1), :] = prod_wide[pl.ds(base + r, 1), :]
         tails_ref[pl.ds(base, unroll), :] = jnp.concatenate(rows, axis=0).astype(BF16)
@@ -253,7 +335,8 @@
         down = raw * scale_col + slope_col * tails_ref[at, :].astype(F32)
         head_grad_ref[at, :] = times_conj(down, rels_ref[at, :].astype(F32))
         grad[at, :] = times_conj(down, heads_ref[at, :].astype(F32))
-    slot_ref[...] = slots
+    for owner in range(BUCKETS):
+        slot_ref[owner] = slots[owner : owner + 1, :]
 
     def step(j, carry):
         for r in range(unroll):
@@ -290,7 +373,7 @@
     def neg_step(j, carry):
         for r in range(unroll):
             for k, one in enumerate(sums):
-                place = pl.ds(neg_ref[k, j * unroll + r], 1)
+                place = pl.ds(neg_ref[k * NEG_PAD + j * unroll + r], 1)
                 one[place, :] = one[place, :] + grad[k, pl.ds(j * unroll + r, 1), :]
         return carry
 
@@ -315,16 +398,16 @@
                 for k, one in enumerate(sums):
                     owner = k * each + s
                     slot = j * unroll + r
-                    place = pl.ds(asked_ref[owner, slot], 1)
-                    term = slope_ref[owner, slot] * wide[pl.ds(owner * LANES + slot, 1), :]
+                    place = pl.ds(asked_ref[owner * LANES + slot], 1)
+                    term = slope_ref[owner * LANES + slot] * wide[pl.ds(owner * LANES + slot, 1), :]
                     one[place, :] = one[place, :] + term
             return j + 1
 
         def more(j):
             at = jnp.minimum(j * unroll, LANES - 1)
-            first = asked_ref[s, at]
+            first = asked_ref[s * LANES + at]
             for k in range(1, 4):
-                first = jnp.minimum(first, asked_ref[k * each + s, at])
+                first = jnp.minimum(first, asked_ref[(k * each + s) * LANES + at])
             return jnp.logical_and(j * unroll < LANES, first < DUMP)
 
         lax.while_loop(more, group, 0)
@@ -341,35 +424,40 @@
     chip = (place // 2).astype(jnp.int32).reshape(1)
     core = (place % 2).astype(jnp.int32).reshape(1)
     pad = jnp.pad(negative_row, ((0, 0), (0, NEG_PAD - negatives)), constant_values=DUMP)
+    pad = pad.reshape(CHIPS * NEG_PAD)
     pack = shape((NEG_PAD + SPAN, LANES), BF16)
     flat = shape((EDGES, LANES), BF16)
     wide = pltpu.VMEM((ROWS + 8, LANES), F32)
 
-    target, request = call(
-        rank_kernel, "rank",
-        (shape((1, EDGES), jnp.int32), shape((BUCKETS, LANES), jnp.int32)), [VM, VM],
+    flags = [pltpu.SemaphoreType.DMA] * 2
+    lists = (BUCKETS, 1, LANES)
+    target, asked = call(
+        rank_kernel, "rank", (shape((1, EDGES), jnp.int32), shape(lists, jnp.int32)), [VM, VM],
+        [pltpu.VMEM(lists, jnp.int32)] + flags, group=0,
     )(tail_owner.reshape(1, EDGES), tail_row.reshape(1, EDGES))
-    asked = lax.all_to_all(request, "bucket", split_axis=0, concat_axis=0, tiled=True)
-
-    p0, p1, p2, p3, product, heads, rels, negs = call(
-        functools.partial(gather_kernel, 32), "gather",
-        (pack, pack, pack, pack, flat, flat, flat, shape((CHIPS, NEG_PAD, LANES), BF16)),
-        [SM, SM, SM, SM, VM, VM],
-        [wide, pltpu.VMEM((RELS, LANES), F32)], size=30000000,
-    )(chip, head_row, relation_id, pad, entity_table, relation_table)
-
-    def along(step):
-        return [(2 * x + c, 2 * ((x + step) % CHIPS) + c) for x in range(CHIPS) for c in range(2)]
-
-    q1 = lax.ppermute(p1, "col", along(1))
-    q2 = lax.ppermute(p2, "col", along(2))
-    q3 = lax.ppermute(p3, "col", along(3))
+    asked = asked.reshape(BUCKETS * LANES)
+    places = target.reshape(EDGES)
 
     found = call(
         functools.partial(found_kernel, 32), "found",
         shape((BUCKETS, LANES, LANES), BF16), [SM, VM], [wide], size=15000000,
     )(asked, entity_table)
     fetched = lax.all_to_all(found, "bucket", split_axis=0, concat_axis=0, tiled=True)
+
+    _, head_late = lax.optimization_barrier((found, head_row))
+    p0, p1, p2, p3, product, heads, rels, negs = call(
+        functools.partial(gather_kernel, 64), "gather",
+        (pack, pack, pack, pack, flat, flat, flat, shape((CHIPS, NEG_PAD, LANES), BF16)),
+        [SM, SM, SM, SM, VM, VM],
+        [wide, pltpu.VMEM((RELS, LANES), F32)], size=30000000,
+    )(chip, head_late, relation_id, pad, entity_table, relation_table)
+
+    def along(step):
+        return [(2 * x + c, 2 * ((x + step) % CHIPS) + c) for x in range(CHIPS) for c in range(2)]
+
+    q1 = lax.ppermute(p1, "col", along(1))
+    q2 = lax.ppermute(p2, "col", along(2))
+    q3 = lax.ppermute(p3, "col", along(3))
 
     half = shape((SPAN // 2, NEG_PAD), F32)
     keep, send = call(score_kernel, "scores", (half, half), [SM, VM, VM, VM, VM],
@@ -380,29 +468,33 @@
         (shape((SPAN // 2, NEG_PAD), BF16), shape((2, SPAN // 2), F32)), [VM, VM],
     )(keep, other)
     weights = lax.all_gather(weight, "col", axis=0, tiled=True)
-    stats = lax.all_gather(stat, "col", axis=0)
 
     tails, partial, slots = call(
         functools.partial(tail_kernel, 32), "tails",
         (flat, shape((1, EDGES), F32), shape((BUCKETS * LANES, LANES), BF16)), [SM, VM, VM],
         [pltpu.VMEM((BUCKETS * LANES, LANES), F32), pltpu.VMEM((BUCKETS * LANES, LANES), F32),
          pltpu.VMEM((EDGES, LANES), F32)], size=15000000,
-    )(target, fetched.reshape(BUCKETS * LANES, LANES), product)
-    positive = lax.psum(partial, "col")
+    )(places, fetched.reshape(BUCKETS * LANES, LANES), product)
     came = lax.all_to_all(slots.reshape(BUCKETS, LANES, LANES), "bucket",
                           split_axis=0, concat_axis=0, tiled=True)
+    positive, stats = call(
+        functools.partial(share_kernel, 8), "share",
+        (shape((1, EDGES), F32), shape((8, 2, SPAN // 2), F32)), [VM, VM],
+        [pltpu.VMEM((8, 1, EDGES), F32), pltpu.SemaphoreType.DMA((2,)),
+         pltpu.SemaphoreType.DMA((2,))], group=1,
+    )(partial, stat)
 
     loss, head_grad, rel_local, slope, scaled = call(
         functools.partial(edge_kernel, 8), "edges",
         (shape((1, EDGES), F32), shape((EDGES, LANES), F32), shape((RELS, LANES), BF16),
-         shape((BUCKETS, LANES), F32), flat),
+         shape(lists, F32), flat),
         [SM] + [VM] * 9,
         [pltpu.VMEM((EDGES, LANES), F32)] + [pltpu.VMEM((RELS, LANES), F32)] * 4,
         size=20000000,
     )(relation_id, target, positive, stats, weights, negs, product, heads, rels, tails)
-    slopes = lax.all_to_all(slope, "bucket", split_axis=0, concat_axis=0, tiled=True)
     rel_parts = lax.all_to_all(rel_local.reshape(BUCKETS, LANES, LANES), "bucket",
                                split_axis=0, concat_axis=0, tiled=True)
+    slopes = call(slope_kernel, "slopes", shape(lists, F32), [VM], flags, group=2)(slope)
 
     part = call(
         functools.partial(entity_kernel, 8, negatives), "entities", shape((ROWS, LANES), F32),
@@ -413,7 +505,7 @@
         functools.partial(owner_kernel, 8), "owners", shape((ROWS, LANES), F32),
         [SM, SM, VM, VM],
         [pltpu.VMEM((BUCKETS * LANES, LANES), F32)] + [wide] * 4, size=30000000,
-    )(asked, slopes, came.reshape(BUCKETS * LANES, LANES), part)
+    )(asked, slopes.reshape(BUCKETS * LANES), came.reshape(BUCKETS * LANES, LANES), part)
     relation_grad = jnp.sum(rel_parts.astype(F32), axis=0)
     return (loss.reshape(EDGES), grad, relation_grad)
 

time: 247 us -> 227 us (0.919); the launches traced: 243 us -> 226 us
  blocking collectives: 103 us -> 36.7 us
  Pallas kernels: 87 us -> 127 us
  waiting for transfers between devices: 18.9 us -> 28.2 us
    pallas_call x2 -> x4, Pallas kernels: 27.5 us -> 67.2 us  [the longest x1 29.2 us: body(): call(slope_kernel, 'slopes', shape(lists, F32), [VM], flags, group=2)(slope)]
    all_to_all x2 -> x0, blocking collectives: 38.4 us -> none  [the longest x1 20 us: body(): lax.all_to_all(request, 'bucket', split_axis=0, concat_axis=0, tiled=True)]
    psum x1 -> x0, blocking collectives: 15.5 us -> none  [body(): positive = lax.psum(partial, 'col')]
    all_gather x1 -> x0, blocking collectives: 12.4 us -> none  [body(): stats = lax.all_gather(stat, 'col', axis=0)]
    all_to_all x1, waiting for transfers between devices: 0.01 us -> 10.4 us  [body(): lax.all_to_all(slots.reshape(BUCKETS, LANES, LANES), 'bucket', split_axis...]
  transfers between devices with their start and end apart: 7 -> 7, of which waited for: 3 -> 4; matrix products, arithmetic and copies ran while one was open for 0% -> 0% of each run, Pallas kernels for 24% -> 36%
where the time goes in v2:
time: 227 us; the launch traced here: 226 us
  Pallas kernels  127 us (56%)
  blocking collectives  36.7 us (16%)
  waiting for transfers between devices  28.2 us (12%)
  starting transfers between devices  16.1 us (7%)
  between operations  14.1 us (6%)
  local copies, waits for them, and re-layouts  3.21 us (1%)
    all_to_all x1, blocking collectives, body(): lax.all_to_all(found, 'bucket', split_axis=0, concat_axis=0, tiled=True)  36.7 us
    pallas_call x1, Pallas kernels, body(): call(slope_kernel, 'slopes', shape(lists, F32), [VM], flags, group=2)(slope)  29.2 us
    pallas_call x1, Pallas kernels, body(): call(rank_kernel, 'rank', (shape((1, EDGES), jnp.int32), shape(lists, jnp...  17.2 us
    pallas_call x1, Pallas kernels, body(): call(functools.partial(entity_kernel, 8, negatives), 'entities', shape((R...  16.1 us
    pallas_call x1, Pallas kernels, body(): call(functools.partial(gather_kernel, 64), 'gather', (pack, pack, pack, p...  13.7 us
    pallas_call x1, Pallas kernels, body(): call(functools.partial(owner_kernel, 8), 'owners', shape((ROWS, LANES), F...  13.4 us
    pallas_call x1, Pallas kernels, body(): call(functools.partial(edge_kernel, 8), 'edges', (shape((1, EDGES), F32),...  10.4 us
    all_to_all x1, waiting for transfers between devices, body(): lax.all_to_all(slots.reshape(BUCKETS, LANES, LANES), 'bucket', split_axis...  10.4 us
  transfers between devices with their start and end apart: 7, of which 4 were waited for; matrix products, arithmetic and copies ran while one was open for 0% of the time, Pallas kernels for 36%

profile of v2, /device:TPU:32, one launch (start us, length us, event | category | flops | bytes accessed | tf_op | source)
XLA Modules:
  0.0 226.2 jit_solution(93983362615091617)
XLA Ops:
  7.2 0.0 all-gather.2.cloned.1.call-start
  7.2 0.7 pad_bitcast_fusion
  7.9 0.6 copy.12
  8.6 17.2 %rank.1 = (s32[1,2048]{1,0:T(1,128)}, s32[32,1,128]{2,1,0:T(1,128)}) custom-call(s32[1,2048]{1,0:T(1,128)} %bitcast.27, s32[1,2048]{1,0:T(1,128)} %bitcast.28), custom_call_target="tpu_custom_call" | custom-call | flops 1000000 | bytes 4000000 | tf_op jit(solution)/shard_map/rank/pallas_call | solution.py:434
  25.8 8.1 %found.1 = bf16[32,128,128]{2,1,0:T(8,128)(2,1)} custom-call(s32[4096]{0:T(1024)} %bitcast.23, bf16[8192,128]{1,0:T(8,128)(2,1)} %table_ref.3), custom_call_target="tpu_custom_call" | custom-call | flops 1000000 | bytes 15000000 | tf_op jit(solution)/shard_map/found/pallas_call | solution.py:441
  33.8 0.0 copy-start
  33.8 13.7 %gather.1 = (bf16[1536,128]{1,0:T(8,128)(2,1)}, bf16[1536,128]{1,0:T(8,128)(2,1)}, bf16[1536,128]{1,0:T(8,128)(2,1)}, bf16[1536,128]{1,0:T(8,128)(2,1)}, bf16[20...) custom-call(s32[1]{0:T(128)} %bitcast.5.chip_ref, ...), custom_call_target="tpu_custom_call" | custom-call | flops 1000000 | bytes 30000000 | tf_op jit(solution)/shard_map/gather/pallas_call | solution.py:448
  47.5 1.5 collective-permute-start
  49.0 2.7 %collective-permute-start.1 = (bf16[1536,128]{1,0:T(8,128)(2,1)}, bf16[1536,128]{1,0:T(8,128)(2,1)S(1)}, u32[]{:S(2)}, u32[]{:S(2)}) collective-permute-start(bf16[1536,128]{1,0:T(8,128)(2,1)} %get-tuple-element.35), channel_id=1, source_target_pairs={{0,4},{1,5},{2,6},{3,7},{4,0},{5,1},{6,2},{7,3},{8,12},{9,13},{10,... | collective-permute-start | bytes 1179656 | tf_op jit(solution)/shard_map/ppermute | solution.py:459
  51.7 1.4 collective-permute-start.2
  53.2 6.8 %collective-permute-done.q1 = bf16[1536,128]{1,0:T(8,128)(2,1)S(1)} collective-permute-done((bf16[1536,128]{1,0:T(8,128)(2,1)}, bf16[1536,128]{1,0:T(8,128)(2,1)S(1)}, u32[]{:S(2)}, u32[]{:S(2)}) %collective-permute-start) | collective-permute-done | bytes 393248 | tf_op jit(solution)/shard_map/ppermute | solution.py:458
  60.0 0.0 copy-start.3
  60.0 8.1 %collective-permute-done.1.q2 = bf16[1536,128]{1,0:T(8,128)(2,1)S(1)} collective-permute-done((bf16[1536,128]{1,0:T(8,128)(2,1)}, bf16[1536,128]{1,0:T(8,128)(2,1)S(1)}, u32[]{:S(2)}, u32[]{:S(2)}) %collective-permute-start.1) | collective-permute-done | bytes 393248 | tf_op jit(solution)/shard_map/ppermute | solution.py:459
  68.1 0.0 copy-start.4
  68.1 0.0 collective-permute-done.2.q3
  68.1 0.0 copy-start.5
  68.1 0.0 copy-done.3
  68.1 0.7 copy-done.4
  68.8 0.1 copy-done.5
  69.0 3.2 %scores.1 = (f32[256,1024]{1,0:T(8,128)}, f32[256,1024]{1,0:T(8,128)}) custom-call(s32[1]{0:T(128)} %bitcast.6.core_ref, bf16[1536,128]{1,0:T(8,128)(2,1)} %get-tuple-element.33.q0, bf16[1536,128]{1,0:T(8,128)(2,1)} %copy-done.3, bf16[1536,128]{1,0:T(8,128)(2,1)} %copy-done.4, bf16[1536,128]{1,0:T(8,128)(2,1)} %copy-done.5), custom_call_target="tpu_custom_call" | custom-call | flops 500000000 | bytes 4000000 | tf_op jit(solution)/shard_map/scores/pallas_call | solution.py:463
  72.1 0.0 collective-permute-start.3
  72.1 2.9 %collective-permute-done.3.other_ref = f32[256,1024]{1,0:T(8,128)S(1)} collective-permute-done((f32[256,1024]{1,0:T(8,128)}, f32[256,1024]{1,0:T(8,128)S(1)}, u32[]{:S(2)}, u32[]{:S(2)}) %collective-permute-start.3) | collective-permute-done | bytes 1048608 | tf_op jit(solution)/shard_map/ppermute | solution.py:465
  75.0 0.0 copy-start.2
  75.0 1.0 copy-done.2
  76.0 2.7 %soft.1 = (bf16[256,1024]{1,0:T(8,128)(2,1)}, f32[2,256]{1,0:T(2,128)}) custom-call(f32[256,1024]{1,0:T(8,128)} %get-tuple-element.37.keep_ref, f32[256,1024]{1,0:T(8,128)} %copy-done.2), custom_call_target="tpu_custom_call" | custom-call | flops 1000000 | bytes 4000000 | tf_op jit(solution)/shard_map/soft/pallas_call | solution.py:466
  78.6 0.0 all-gather.2.cloned.1.call-update
  78.6 0.0 copy-done
  78.6 36.7 %all_to_all.15 = bf16[32,128,128]{2,1,0:T(8,128)(2,1)} all-to-all(bf16[32,128,128]{2,1,0:T(8,128)(2,1)S(1)} %copy-done), channel_id=1, replica_groups=mesh['bucket'=32,'col'=8] {'bucket'}, dimensions={0} | all-to-all | bytes 2097152 | tf_op jit(solution)/shard_map/all_to_all | solution.py:445
  115.4 6.1 %tails.1 = (bf16[2048,128]{1,0:T(8,128)(2,1)}, f32[1,2048]{1,0:T(1,128)}, bf16[4096,128]{1,0:T(8,128)(2,1)}) custom-call(s32[2048]{0:T(1024)} %bitcast.26, bf16[4096,128]{1,0:T(8,128)(2,1)} %bitcast.18, bf16[2048,128]{1,0:T(8,128)(2,1)} %get-tuple-element.31.product_ref), custom_call_target="tpu_custom_call" | custom-call | flops 1000000 | bytes 15000000 | tf_op jit(solution)/shard_map/tails/pallas_call | solution.py:472
  121.4 5.2 %all-to-all-start.1 = ((bf16[32,128,128]{2,1,0:T(8,128)(2,1)}), bf16[32,128,128]{2,1,0:T(8,128)(2,1)S(1)}, u32[]{:S(2)}, u32[]{:S(2)}) async-start(bf16[32,128,128]{2,1,0:T(8,128)(2,1)} %bitcast.19), calls=%async_computation.1 | async-start | bytes 2097152 | tf_op jit(solution)/shard_map/all_to_all | solution.py:478
  126.7 7.2 %share.1 = (f32[1,2048]{1,0:T(1,128)}, f32[8,2,256]{2,1,0:T(2,128)}) custom-call(f32[1,2048]{1,0:T(1,128)} %get-tuple-element.32.partial_ref, f32[2,256]{1,0:T(2,128)} %get-tuple-element.39.stat_ref), custom_call_target="tpu_custom_call" | custom-call | flops 1000000 | bytes 4000000 | tf_op jit(solution)/shard_map/share/pallas_call | solution.py:480
  133.8 0.0 all-gather.2.cloned.1.call-done.weight_ref
  133.9 10.4 %edges.1 = (f32[1,2048]{1,0:T(1,128)}, f32[2048,128]{1,0:T(8,128)}, bf16[4096,128]{1,0:T(8,128)(2,1)}, f32[32,1,128]{2,1,0:T(1,128)}, bf16[2048,128]{1,0:T(8,128)(2,1)}) custom-call(s32[2048]{0:T(1024)} %rel_ref.3, s32[1,2048]{1,0:T(1,128)} %get-tuple-element.28.target_ref, f32[1,2048]{1,0:T(1,128)} %get-tuple-element.40.positive_ref, ...), custom_call_target="tpu_custom_call" | custom-call | flops 1000000 | bytes 20000000 | tf_op jit(solution)/shard_map/edges/pallas_call | solution.py:487
  144.3 10.4 %all-to-all-done.1 = bf16[32,128,128]{2,1,0:T(8,128)(2,1)S(1)} async-done(((bf16[32,128,128]{2,1,0:T(8,128)(2,1)}), bf16[32,128,128]{2,1,0:T(8,128)(2,1)S(1)}, u32[]{:S(2)}, u32[]{:S(2)}) %all-to-all-start.1) | async-done | bytes 1048608 | tf_op jit(solution)/shard_map/all_to_all | solution.py:478
  154.7 0.0 copy-start.1
  154.7 5.2 %all-to-all-start.2 = ((bf16[32,128,128]{2,1,0:T(8,128)(2,1)}), bf16[32,128,128]{2,1,0:T(8,128)(2,1)S(1)}, u32[]{:S(2)}, u32[]{:S(2)}) async-start(bf16[32,128,128]{2,1,0:T(8,128)(2,1)} %bitcast.20), calls=%async_computation.2 | async-start | bytes 2097152 | tf_op jit(solution)/shard_map/all_to_all | solution.py:495
  159.8 29.2 %slopes.1 = f32[32,1,128]{2,1,0:T(1,128)} custom-call(f32[32,1,128]{2,1,0:T(1,128)} %get-tuple-element.48.slope_ref), custom_call_target="tpu_custom_call" | custom-call | flops 1000000 | bytes 4000000 | tf_op jit(solution)/shard_map/slopes/pallas_call | solution.py:497
  189.0 16.1 %entities.1.part_ref = f32[8192,128]{1,0:T(8,128)} custom-call(s32[2048]{0:T(1024)} %head_ref.2, s32[4096]{0:T(1024)} %bitcast.22, bf16[2048,1024]{1,0:T(8,128)(2,1)} %all-gather.2.cloned.1.call-done.weight_ref, bf16[2048,128]{1,0:T(8,128)(2,1)} %get-tuple-element.50.scaled_ref, f32[2048,128]{1,0:T(8,128)} %get-tuple-element.51.head_grad_ref), custom_call_target="tpu_custom_call" | custom-call | flops 1000000 | bytes 40000000 | tf_op jit(solution)/shard_map/entities/pallas_call | solution.py:499
  205.1 0.0 copy-done.1
  205.1 13.4 %owners.1 = f32[8192,128]{1,0:T(8,128)} custom-call(s32[4096]{0:T(1024)} %bitcast.24, f32[4096]{0:T(1024)} %bitcast.25, bf16[4096,128]{1,0:T(8,128)(2,1)} %bitcast.17, f32[8192,128]{1,0:T(8,128)} %entities.1.part_ref), custom_call_target="tpu_custom_call" | custom-call | flops 1000000 | bytes 30000000 | tf_op jit(solution)/shard_map/owners/pallas_call | solution.py:504
  218.5 0.0 all-to-all-done.2
  218.6 0.8 convert_reduce_fusion
Async XLA Ops:
  7.2 126.7 %all-gather.2.cloned.1.call-start = ((), (), s32[]{:S(2)}) async-start(), calls=%async_computation.3 | async-start | bytes 4718592 | tf_op jit(solution)/shard_map/all_gather | solution.py:470
  33.8 44.8 %copy-start = (bf16[32,128,128]{2,1,0:T(8,128)(2,1)S(1)}, bf16[32,128,128]{2,1,0:T(8,128)(2,1)}, u32[]{:S(2)}) copy-start(bf16[32,128,128]{2,1,0:T(8,128)(2,1)} %found.1) | copy-start | bytes 3145732
  47.5 12.5 %collective-permute-start = (bf16[1536,128]{1,0:T(8,128)(2,1)}, bf16[1536,128]{1,0:T(8,128)(2,1)S(1)}, u32[]{:S(2)}, u32[]{:S(2)}) collective-permute-start(bf16[1536,128]{1,0:T(8,128)(2,1)} %get-tuple-element.34), channel_id=1, source_target_pairs={{0,2},{1,3},{2,4},{3,5},{4,6},{5,7},{6,0},{7,1},{8,10},{9,11},{10,... | collective-permute-start | bytes 1179656 | tf_op jit(solution)/shard_map/ppermute | solution.py:458
  49.0 19.1 %collective-permute-start.1 = (bf16[1536,128]{1,0:T(8,128)(2,1)}, bf16[1536,128]{1,0:T(8,128)(2,1)S(1)}, u32[]{:S(2)}, u32[]{:S(2)}) collective-permute-start(bf16[1536,128]{1,0:T(8,128)(2,1)} %get-tuple-element.35), channel_id=1, source_target_pairs={{0,4},{1,5},{2,6},{3,7},{4,0},{5,1},{6,2},{7,3},{8,12},{9,13},{10,... | collective-permute-start | bytes 1179656 | tf_op jit(solution)/shard_map/ppermute | solution.py:459
  51.7 16.3 %collective-permute-start.2 = (bf16[1536,128]{1,0:T(8,128)(2,1)}, bf16[1536,128]{1,0:T(8,128)(2,1)S(1)}, u32[]{:S(2)}, u32[]{:S(2)}) collective-permute-start(bf16[1536,128]{1,0:T(8,128)(2,1)} %get-tuple-element.36), channel_id=1, source_target_pairs={{0,6},{1,7},{2,0},{3,1},{4,2},{5,3},{6,4},{7,5},{8,14},{9,15},{10,... | collective-permute-start | bytes 1179656 | tf_op jit(solution)/shard_map/ppermute | solution.py:460
  60.0 8.1 %copy-start.3 = (bf16[1536,128]{1,0:T(8,128)(2,1)}, bf16[1536,128]{1,0:T(8,128)(2,1)S(1)}, u32[]{:S(2)}) copy-start(bf16[1536,128]{1,0:T(8,128)(2,1)S(1)} %collective-permute-done.q1) | copy-start | bytes 1179652
  68.1 0.8 copy-start.4
  68.1 0.9 copy-start.5
  72.1 2.9 %collective-permute-start.3 = (f32[256,1024]{1,0:T(8,128)}, f32[256,1024]{1,0:T(8,128)S(1)}, u32[]{:S(2)}, u32[]{:S(2)}) collective-permute-start(f32[256,1024]{1,0:T(8,128)} %get-tuple-element.38), channel_id=1, source_target_pairs={{0,1},{1,0},{2,3},{3,2},{4,5},{5,4},{6,7},{7,6},{8,9},{9,8},{10,11... | collective-permute-start | bytes 3145736 | tf_op jit(solution)/shard_map/ppermute | solution.py:465
  75.0 1.0 copy-start.2
  121.4 33.2 %all-to-all-start.1 = ((bf16[32,128,128]{2,1,0:T(8,128)(2,1)}), bf16[32,128,128]{2,1,0:T(8,128)(2,1)S(1)}, u32[]{:S(2)}, u32[]{:S(2)}) async-start(bf16[32,128,128]{2,1,0:T(8,128)(2,1)} %bitcast.19), calls=%async_computation.1 | async-start | bytes 2097152 | tf_op jit(solution)/shard_map/all_to_all | solution.py:478
  154.7 50.5 %copy-start.1 = (bf16[32,128,128]{2,1,0:T(8,128)(2,1)}, bf16[32,128,128]{2,1,0:T(8,128)(2,1)S(1)}, u32[]{:S(2)}) copy-start(bf16[32,128,128]{2,1,0:T(8,128)(2,1)S(1)} %all-to-all-done.1) | copy-start | bytes 3145732
  154.7 63.9 %all-to-all-start.2 = ((bf16[32,128,128]{2,1,0:T(8,128)(2,1)}), bf16[32,128,128]{2,1,0:T(8,128)(2,1)S(1)}, u32[]{:S(2)}, u32[]{:S(2)}) async-start(bf16[32,128,128]{2,1,0:T(8,128)(2,1)} %bitcast.20), calls=%async_computation.2 | async-start | bytes 2097152 | tf_op jit(solution)/shard_map/all_to_all | solution.py:495
Sparse Core Ops, SparseCore 0:
  78.8 33.3 all-gather.1

commit v3 on v2

v3 whole, which is shorter than its diff:
```python
import functools

import jax
import jax.numpy as jnp
from jax import lax
from jax.experimental import pallas as pl
from jax.experimental.pallas import tpu as pltpu
from jax.sharding import PartitionSpec as P

LANES = 128
SPAN = 512
NEG_PAD = 1024
ROWS = 8192
DUMP = 8192
RELS = 4096
EDGES = 2048
BUCKETS = 32
COLS = 8
UNROLL = 64
CHIPS = 4
F32 = jnp.float32
BF16 = jnp.bfloat16
VM = pl.BlockSpec(memory_space=pltpu.VMEM)
SM = pl.BlockSpec(memory_space=pltpu.SMEM)
NT = (((1,), (1,)), ((), ()))
TN = (((0,), (0,)), ((), ()))


def call(kernel, name, outs, ins, scratch=(), flops=1000000, size=4000000, group=None):
    remote = {} if group is None else dict(collective_id=group, has_side_effects=True)
    return pl.pallas_call(
        kernel,
        name=name,
        out_shape=outs,
        in_specs=ins,
        out_specs=jax.tree.map(lambda _: VM, outs),
        scratch_shapes=scratch,
        compiler_params=pltpu.CompilerParams(vmem_limit_bytes=56 << 20, **remote),
        cost_estimate=pl.CostEstimate(flops=flops, bytes_accessed=size, transcendentals=0),
    )


def shape(dims, kind):
    return jax.ShapeDtypeStruct(dims, kind)


def iota(dims, axis):
    return lax.broadcasted_iota(jnp.int32, dims, axis)


def to_column(row):
    size = row.shape[1]
    same = iota((size, size), 0) == iota((size, size), 1)
    return jnp.sum(jnp.where(same, row, 0.0), axis=1, keepdims=True)


def to_row(column):
    size = column.shape[0]
    same = iota((size, size), 0) == iota((size, size), 1)
    return jnp.sum(jnp.where(same, column, 0.0), axis=0, keepdims=True)


def swap_halves(value):
    return pltpu.roll(value, LANES // 2, 1)


def times(left, right):
    lane = iota(left.shape, 1)
    first = lane < LANES // 2
    turned = swap_halves(right)
    real = jnp.where(first, right, turned)
    imag = jnp.where(first, -turned, right)
    return left * real + swap_halves(left) * imag


def times_conj(left, right):
    lane = iota(left.shape, 1)
    first = lane < LANES // 2
    turned = swap_halves(right)
    real = jnp.where(first, right, turned)
    imag = jnp.where(first, turned, -right)
    return left * real + swap_halves(left) * imag


def greet(axis, count):
    me = lax.axis_index(axis)
    barrier = pltpu.get_barrier_semaphore()

    def tell(i, carry):
        peer = lax.rem(me + i, count)
        pl.semaphore_signal(barrier, inc=1, device_id={axis: peer},
                            device_id_type=pl.DeviceIdType.MESH)
        return carry

    lax.fori_loop(1, count, tell, 0)
    pl.semaphore_wait(barrier, count - 1)


def spread(axis, count, src, dst, send_sem, recv_sem):
    me = lax.axis_index(axis)

    def send(i, carry):
        peer = lax.rem(me + i, count)
        pltpu.make_async_remote_copy(
            src_ref=src.at[peer], dst_ref=dst.at[me], send_sem=send_sem, recv_sem=recv_sem,
            device_id={axis: peer}, device_id_type=pl.DeviceIdType.MESH).start()
        return carry

    lax.fori_loop(1, count, send, 0)


def settle(axis, count, src, dst, send_sem, recv_sem):
    me = lax.axis_index(axis)
    rest = pl.ds(0, count - 1)
    pltpu.make_async_remote_copy(
        src_ref=src.at[rest], dst_ref=dst.at[rest], send_sem=send_sem, recv_sem=recv_sem,
        device_id={axis: lax.rem(me + 1, count)}, device_id_type=pl.DeviceIdType.MESH).wait()


def slope_kernel(slope_ref, out_ref, send_sem, recv_sem):
    greet("bucket", BUCKETS)
    spread("bucket", BUCKETS, slope_ref, out_ref, send_sem, recv_sem)
    me = lax.axis_index("bucket")
    out_ref[me] = slope_ref[me]
    settle("bucket", BUCKETS, slope_ref, out_ref, send_sem, recv_sem)


def load_table(table_ref, wide_ref, rows):
    wide_ref[0:rows, :] = table_ref[...].astype(F32)


def to(peers):
    return dict(device_id=peers, device_id_type=pl.DeviceIdType.MESH)


def forward_kernel(negatives, head_ref, rel_ref, neg_ref, owner_ref, row_ref, table_ref, rtable_ref,
                   target_ref, asked_ref, came_ref, tails_ref, product_ref, heads_ref, rels_ref,
                   negs_ref, weights_ref, stats_ref, positive_ref,
                   wide, rwide, prod_wide, tail_wide, request, inverse, found, fetched, slots,
                   pack, got, keep, send, other, parts, asked_s, target_s, inverse_s,
                   local_sem, bucket_send, bucket_recv, pack_send, pack_recv, swap_send, swap_recv,
                   weight_send, weight_recv, near_send, near_recv, part_send, part_recv):
    me = lax.axis_index("bucket")
    place = lax.axis_index("col")
    chip, core = place // 2, lax.rem(place, 2)
    near = {"col": 2 * chip + (1 - core)}

    barrier = pltpu.get_barrier_semaphore()
    for axis, count in (("bucket", BUCKETS), ("col", COLS)):
        def tell(i, carry):
            peer = lax.rem(lax.axis_index(axis) + i, count)
            pl.semaphore_signal(barrier, inc=1, **to({axis: peer}))
            return carry

        lax.fori_loop(1, count, tell, 0)
    load_table(table_ref, wide, ROWS)
    load_table(rtable_ref, rwide, RELS)
    wide[ROWS : ROWS + 8, :] = jnp.zeros((8, LANES), F32)
    prod_wide[EDGES : EDGES + 8, :] = jnp.zeros((8, LANES), F32)

    def pack_copy(step):
        return pltpu.make_async_remote_copy(
            src_ref=pack.at[step], dst_ref=got.at[step], send_sem=pack_send.at[step],
            recv_sem=pack_recv.at[step], **to({"col": 2 * lax.rem(chip + step, CHIPS) + core}))

    def fill(step):
        span = lax.rem(chip + step, CHIPS)

        def edge_step(j, carry):
            base = pl.multiple_of(span * SPAN + j * UNROLL, UNROLL)
            head = jnp.concatenate(
                [wide[pl.ds(head_ref[base + r], 1), :] for r in range(UNROLL)], axis=0)
            rel = jnp.concatenate(
                [rwide[pl.ds(rel_ref[base + r], 1), :] for r in range(UNROLL)], axis=0)
            product = times(head, rel).astype(BF16)
            at = pl.ds(base, UNROLL)
            pack[step, pl.ds(pl.multiple_of(NEG_PAD + j * UNROLL, UNROLL), UNROLL), :] = product
            product_ref[at, :] = product
            prod_wide[at, :] = product.astype(F32)
            heads_ref[at, :] = head.astype(BF16)
            rels_ref[at, :] = rel.astype(BF16)
            return carry

        lax.fori_loop(0, SPAN // UNROLL, edge_step, 0)

        def neg_step(j, carry):
            base = pl.multiple_of(j * UNROLL, UNROLL)
            start = span * NEG_PAD + j * UNROLL
            rows = jnp.concatenate(
                [wide[pl.ds(neg_ref[start + r], 1), :] for r in range(UNROLL)],
                axis=0).astype(BF16)
            pack[step, pl.ds(base, UNROLL), :] = rows
            negs_ref[span, pl.ds(base, UNROLL), :] = rows
            return carry

        lax.fori_loop(0, NEG_PAD // UNROLL, neg_step, 0)

    fill(2)
    pl.semaphore_wait(barrier, BUCKETS + COLS - 2)

    pack_copy(2).start()
    fill(1)
    pack_copy(1).start()
    fill(3)
    pack_copy(3).start()

    lower = (iota((LANES, LANES), 0) <= iota((LANES, LANES), 1)).astype(BF16)
    lane = iota((LANES, LANES), 1).astype(F32)
    before = jnp.zeros((BUCKETS, 1), F32)
    nothing = jnp.zeros((BUCKETS, LANES), F32)
    high, low, first, last = nothing, nothing, nothing, nothing
    for block in range(EDGES // LANES):
        at = slice(block * LANES, (block + 1) * LANES)
        owner = owner_ref[:, at]
        row = row_ref[:, at]
        mine = iota((BUCKETS, LANES), 0) == owner
        hit = mine.astype(F32).astype(BF16)
        count = jnp.dot(hit, lower, preferred_element_type=F32)
        ranks = jnp.where(mine, count + before - 1.0, 0.0)
        rank = jnp.sum(ranks, axis=0, keepdims=True).astype(jnp.int32)
        before = before + count[:, LANES - 1 : LANES]
        target_ref[block] = jnp.clip(owner * LANES + rank, 0, BUCKETS * LANES - 1)
        slot = iota((LANES, LANES), 0) == rank

        def placed(values):
            spread_out = jnp.where(slot, values, 0.0).astype(BF16)
            return lax.dot_general(hit, spread_out, NT, preferred_element_type=F32)

        high = high + placed((row >> 7).astype(F32))
        low = low + placed((row & 127).astype(F32))
        first = first + float(block) * placed(jnp.ones((1, LANES), F32))
        last = last + placed(lane)
    used = iota((BUCKETS, LANES), 1).astype(F32) < before
    rows = jnp.where(used, high * 128.0 + low, float(DUMP)).astype(jnp.int32)
    edges = jnp.where(used, first * 128.0 + last, float(EDGES)).astype(jnp.int32)
    for owner in range(BUCKETS):
        request[owner] = jnp.clip(rows[owner : owner + 1, :], 0, DUMP)
        inverse[owner] = jnp.clip(edges[owner : owner + 1, :], 0, EDGES)

    spread("bucket", BUCKETS, request, asked_ref, bucket_send.at[0], bucket_recv.at[0])
    copies = [pltpu.make_async_copy(target_ref, target_s, local_sem.at[0]),
              pltpu.make_async_copy(inverse, inverse_s, local_sem.at[1])]
    for copy in copies:
        copy.start()
    asked_ref[me] = request[me]

    fill(0)

    settle("bucket", BUCKETS, request, asked_ref, bucket_send.at[0], bucket_recv.at[0])
    copy = pltpu.make_async_copy(asked_ref, asked_s, local_sem.at[2])
    copy.start()
    copy.wait()

    def bucket_copy(src, dst, which, peer):
        return pltpu.make_async_remote_copy(
            src_ref=src.at[peer], dst_ref=dst.at[me], send_sem=bucket_send.at[which],
            recv_sem=bucket_recv.at[which], **to({"bucket": peer}))

    def take(source, index, out, s):
        for part in range(LANES // UNROLL):
            rows = jnp.concatenate(
                [source[pl.ds(index[s, 0, part * UNROLL + r], 1), :] for r in range(UNROLL)],
                axis=0)
            out[s, part * UNROLL : (part + 1) * UNROLL, :] = rows.astype(BF16)

    def find(i, carry):
        peer = lax.rem(me + i, BUCKETS)
        take(wide, asked_s, found, peer)
        bucket_copy(found, fetched, 1, peer).start()
        return carry

    lax.fori_loop(1, BUCKETS, find, 0)
    take(wide, asked_s, fetched, me)

    for step in range(1, CHIPS):
        pack_copy(step).wait()
    halves = SPAN // 2
    swap = pltpu.make_async_remote_copy(
        src_ref=send, dst_ref=other, send_sem=swap_send, recv_sem=swap_recv, **to(near))

    def score(half, out):
        at = pl.ds(pl.multiple_of(NEG_PAD + half * halves, halves), halves)
        parts_of = [pack.at[0]] + [got.at[step] for step in range(1, CHIPS)]
        left = jnp.concatenate([q[at, :] for q in parts_of], axis=1)

        def piece(i, carry):
            cut = pl.ds(pl.multiple_of(i * 256, 256), 256)
            right = jnp.concatenate([q[cut, :] for q in parts_of], axis=1)
            out[:, cut] = lax.dot_general(left, right, NT, preferred_element_type=F32)
            return carry

        lax.fori_loop(0, NEG_PAD // 256, piece, 0)

    score(1 - core, send)
    swap.start()
    score(core, keep)
    swap.wait()

    for block in range(halves // LANES):
        at = slice(block * LANES, (block + 1) * LANES)
        scores = keep[at, :] + other[at, :]
        real = iota((LANES, NEG_PAD), 1) < negatives
        scores = jnp.where(real, scores, -jnp.inf)
        top = jnp.max(scores, axis=1, keepdims=True)
        expo = jnp.exp(scores - top)
        weights_ref[place, at, :] = expo.astype(BF16)
        stats_ref[place, 0:1, at] = to_row(top)
        stats_ref[place, 1:2, at] = to_row(jnp.sum(expo, axis=1, keepdims=True))

    def weight_copy(step):
        return pltpu.make_async_remote_copy(
            src_ref=weights_ref.at[place], dst_ref=weights_ref.at[place],
            send_sem=weight_send.at[step], recv_sem=weight_recv.at[step],
            **to({"col": 2 * lax.rem(chip + step, CHIPS) + core}))

    def near_copy(step, side):
        piece = 2 * lax.rem(chip - step + CHIPS, CHIPS) + side
        return pltpu.make_async_remote_copy(
            src_ref=weights_ref.at[piece], dst_ref=weights_ref.at[piece],
            send_sem=near_send.at[step], recv_sem=near_recv.at[step], **to(near))

    def weight_came(step):
        piece = 2 * lax.rem(chip - step + CHIPS, CHIPS) + core
        pltpu.make_async_remote_copy(
            src_ref=weights_ref.at[piece], dst_ref=weights_ref.at[piece],
            send_sem=weight_send.at[step], recv_sem=weight_recv.at[step], **to(near)).wait_recv()

    for step in range(1, CHIPS):
        weight_copy(step).start()
    near_copy(0, core).start()

    for copy in copies:
        copy.wait()

    def give(i, carry):
        peer = lax.rem(me + i, BUCKETS)
        take(prod_wide, inverse_s, slots, peer)
        bucket_copy(slots, came_ref, 2, peer).start()
        return carry

    lax.fori_loop(1, BUCKETS, give, 0)
    take(prod_wide, inverse_s, came_ref, me)

    settle("bucket", BUCKETS, found, fetched, bucket_send.at[1], bucket_recv.at[1])
    tail_wide[...] = fetched[...].reshape(BUCKETS * LANES, LANES).astype(F32)

    def tail_step(block, carry):
        base = pl.multiple_of(block * LANES, LANES)
        for part in range(LANES // UNROLL):
            rows = jnp.concatenate(
                [tail_wide[pl.ds(target_s[block, 0, part * UNROLL + r], 1), :]
                 for r in range(UNROLL)], axis=0)
            tails_ref[pl.ds(pl.multiple_of(base + part * UNROLL, UNROLL), UNROLL), :] = (
                rows.astype(BF16))
        at = pl.ds(base, LANES)
        both = tails_ref[at, :].astype(F32) * prod_wide[at, :]
        parts[place, block] = to_row(jnp.sum(both, axis=1, keepdims=True))
        return carry

    lax.fori_loop(0, EDGES // LANES, tail_step, 0)

    def part_copy(k, ref, peer):
        return pltpu.make_async_remote_copy(
            src_ref=ref.at[place], dst_ref=ref.at[place], send_sem=part_send.at[k],
            recv_sem=part_recv.at[k], **to({"col": peer}))

    def tell_parts(i, carry):
        peer = lax.rem(place + i, COLS)
        part_copy(0, parts, peer).start()
        part_copy(1, stats_ref, peer).start()
        return carry

    lax.fori_loop(1, COLS, tell_parts, 0)

    for step in range(1, CHIPS):
        weight_came(step)
        near_copy(step, core).start()
    rest = pl.ds(0, COLS - 1)
    for k, ref in enumerate((parts, stats_ref)):
        pltpu.make_async_remote_copy(
            src_ref=ref.at[rest], dst_ref=ref.at[rest], send_sem=part_send.at[k],
            recv_sem=part_recv.at[k], **to(near)).wait()
    total = parts[0]
    for k in range(1, COLS):
        total = total + parts[k]
    positive_ref[...] = total
    for step in range(CHIPS):
        near_copy(step, core).wait_send()
        near_copy(step, 1 - core).wait_recv()
    for step in range(1, CHIPS):
        weight_copy(step).wait_send()
    settle("bucket", BUCKETS, slots, came_ref, bucket_send.at[2], bucket_recv.at[2])


def edge_kernel(unroll, rel_ref, target_ref, positive_ref, stat_ref, weight_ref, negs_ref,
                product_ref, heads_ref, rels_ref, tails_ref,
                loss_ref, head_grad_ref, rel_grad_ref, slot_ref, scaled_ref,
                grad, a0, a1, a2, a3):
    sums = (a0, a1, a2, a3)
    for one in sums:
        one[...] = jnp.zeros_like(one)
    slots = jnp.zeros((BUCKETS, LANES), F32)
    half = SPAN // 2
    for block in range(EDGES // LANES):
        at = slice(block * LANES, (block + 1) * LANES)
        part, inner = block // 2, (block % 2) * LANES
        high = stat_ref[part, 0:1, inner : inner + LANES]
        mass = stat_ref[part, 1:2, inner : inner + LANES]
        positive = positive_ref[block]
        top = jnp.maximum(high, positive)
        shrink = jnp.exp(high - top)
        expo = jnp.exp(positive - top)
        total = mass * shrink + expo
        scale = shrink / total
        slope = expo / total - 1.0
        loss_ref[:, at] = top + jnp.log(total) - positive
        target = target_ref[block]
        hit = (iota((BUCKETS, LANES), 0) == (target >> 7)).astype(F32).astype(BF16)
        slot = iota((LANES, LANES), 0) == (target & 127)
        rest = slope
        for _ in range(3):
            piece = rest.astype(BF16)
            spread = jnp.where(slot, piece.astype(F32), 0.0).astype(BF16)
            slots = slots + lax.dot_general(hit, spread, NT, preferred_element_type=F32)
            rest = rest - piece.astype(F32)
        scale_col = to_column(scale)
        slope_col = to_column(slope)
        scaled_ref[at, :] = (product_ref[at, :].astype(F32) * scale_col).astype(BF16)
        raw = jnp.dot(weight_ref[at, :], negs_ref[block // 4], preferred_element_type=F32)
        down = raw * scale_col + slope_col * tails_ref[at, :].astype(F32)
        head_grad_ref[at, :] = times_conj(down, rels_ref[at, :].astype(F32))
        grad[at, :] = times_conj(down, heads_ref[at, :].astype(F32))
    for owner in range(BUCKETS):
        slot_ref[owner] = slots[owner : owner + 1, :]

    def step(j, carry):
        for r in range(unroll):
            for k, one in enumerate(sums):
                edge = k * SPAN + j * unroll + r
                place = pl.ds(rel_ref[edge], 1)
                one[place, :] = one[place, :] + grad[pl.ds(edge, 1), :]
        return carry

    lax.fori_loop(0, SPAN // unroll, step, 0)
    rel_grad_ref[...] = ((a0[...] + a1[...]) + (a2[...] + a3[...])).astype(BF16)


def entity_kernel(unroll, negatives, head_ref, neg_ref, weight_ref, scaled_ref, head_grad_ref,
                  out_ref, grad, a0, a1, a2, a3):
    sums = (a0, a1, a2, a3)
    for one in sums:
        one[...] = jnp.zeros_like(one)
    for span in range(CHIPS):
        at = slice(span * SPAN, (span + 1) * SPAN)
        grad[span] = lax.dot_general(
            weight_ref[at, :], scaled_ref[at, :], TN, preferred_element_type=F32)

    def edge_step(j, carry):
        for r in range(unroll):
            for k, one in enumerate(sums):
                edge = k * SPAN + j * unroll + r
                place = pl.ds(head_ref[edge], 1)
                one[place, :] = one[place, :] + head_grad_ref[pl.ds(edge, 1), :]
        return carry

    lax.fori_loop(0, SPAN // unroll, edge_step, 0)

    def neg_step(j, carry):
        for r in range(unroll):
            for k, one in enumerate(sums):
                place = pl.ds(neg_ref[k * NEG_PAD + j * unroll + r], 1)
                one[place, :] = one[place, :] + grad[k, pl.ds(j * unroll + r, 1), :]
        return carry

    lax.fori_loop(0, negatives // unroll, neg_step, 0)
    total = (a0[0:ROWS, :] + a1[0:ROWS, :]) + (a2[0:ROWS, :] + a3[0:ROWS, :])
    out_ref[...] = total


def owner_kernel(unroll, asked_ref, slope_ref, came_ref, part_ref, out_ref,
                 wide, a0, a1, a2, a3):
    sums = (a0, a1, a2, a3)
    for one in sums[1:]:
        one[...] = jnp.zeros_like(one)
    a0[0:ROWS, :] = part_ref[...]
    a0[ROWS : ROWS + 8, :] = jnp.zeros((8, LANES), F32)
    wide[...] = came_ref[...].astype(F32)
    each = BUCKETS // 4

    def source(s, carry):
        def group(j):
            for r in range(unroll):
                for k, one in enumerate(sums):
                    owner = k * each + s
                    slot = j * unroll + r
                    place = pl.ds(asked_ref[owner * LANES + slot], 1)
                    term = slope_ref[owner * LANES + slot] * wide[pl.ds(owner * LANES + slot, 1), :]
                    one[place, :] = one[place, :] + term
            return j + 1

        def more(j):
            at = jnp.minimum(j * unroll, LANES - 1)
            first = asked_ref[s * LANES + at]
            for k in range(1, 4):
                first = jnp.minimum(first, asked_ref[(k * each + s) * LANES + at])
            return jnp.logical_and(j * unroll < LANES, first < DUMP)

        lax.while_loop(more, group, 0)
        return carry

    lax.fori_loop(0, each, source, 0)
    total = (a0[0:ROWS, :] + a1[0:ROWS, :]) + (a2[0:ROWS, :] + a3[0:ROWS, :])
    out_ref[...] = total


def body(entity_table, relation_table, head_row, relation_id, tail_owner, tail_row, negative_row):
    negatives = negative_row.shape[1]
    pad = jnp.pad(negative_row, ((0, 0), (0, NEG_PAD - negatives)), constant_values=DUMP)
    pad = pad.reshape(CHIPS * NEG_PAD)
    flat = shape((EDGES, LANES), BF16)
    wide = pltpu.VMEM((ROWS + 8, LANES), F32)
    lists = (BUCKETS, 1, LANES)
    blocks = (EDGES // LANES, 1, LANES)
    grid = (BUCKETS, LANES, LANES)
    half = pltpu.VMEM((SPAN // 2, NEG_PAD), F32)
    packs = pltpu.VMEM((CHIPS, NEG_PAD + SPAN, LANES), BF16)
    flag = pltpu.SemaphoreType.DMA
    (target, asked, came, tails, product, heads, rels, negs, weights, stats, positive) = call(
        functools.partial(forward_kernel, negatives), "forward",
        (shape(blocks, jnp.int32), shape(lists, jnp.int32), shape(grid, BF16), flat, flat, flat,
         flat, shape((CHIPS, NEG_PAD, LANES), BF16), shape((COLS, SPAN // 2, NEG_PAD), BF16),
         shape((COLS, 2, SPAN // 2), F32), shape(blocks, F32)),
        [SM] * 3 + [VM] * 4,
        [wide, pltpu.VMEM((RELS, LANES), F32), pltpu.VMEM((EDGES + 8, LANES), F32),
         pltpu.VMEM((BUCKETS * LANES, LANES), F32), pltpu.VMEM(lists, jnp.int32),
         pltpu.VMEM(lists, jnp.int32), pltpu.VMEM(grid, BF16), pltpu.VMEM(grid, BF16),
         pltpu.VMEM(grid, BF16), packs, packs, half, half, half,
         pltpu.VMEM((COLS,) + blocks, F32), pltpu.SMEM(lists, jnp.int32),
         pltpu.SMEM(blocks, jnp.int32), pltpu.SMEM(lists, jnp.int32),
         flag((3,)), flag((3,)), flag((3,)), flag((CHIPS,)), flag((CHIPS,)), flag, flag,
         flag((CHIPS,)), flag((CHIPS,)), flag((CHIPS,)), flag((CHIPS,)), flag((2,)), flag((2,))],
        flops=600000000, size=40000000, group=0,
    )(head_row, relation_id, pad, tail_owner.reshape(1, EDGES), tail_row.reshape(1, EDGES),
      entity_table, relation_table)
    asked = asked.reshape(BUCKETS * LANES)
    weights = weights.reshape(EDGES, NEG_PAD)
    flags = [flag] * 2

    loss, head_grad, rel_local, slope, scaled = call(
        functools.partial(edge_kernel, 8), "edges",
        (shape((1, EDGES), F32), shape((EDGES, LANES), F32), shape((RELS, LANES), BF16),
         shape(lists, F32), flat),
        [SM] + [VM] * 9,
        [pltpu.VMEM((EDGES, LANES), F32)] + [pltpu.VMEM((RELS, LANES), F32)] * 4,
        size=20000000,
    )(relation_id, target, positive, stats, weights, negs, product, heads, rels, tails)
    slopes = call(slope_kernel, "slopes", shape(lists, F32), [VM], flags, group=1)(slope)
    _, rel_local = lax.optimization_barrier((slopes, rel_local))
    rel_parts = lax.all_to_all(rel_local.reshape(BUCKETS, LANES, LANES), "bucket",
                               split_axis=0, concat_axis=0, tiled=True)

    part = call(
        functools.partial(entity_kernel, 8, negatives), "entities", shape((ROWS, LANES), F32),
        [SM, SM, VM, VM, VM],
        [pltpu.VMEM((CHIPS, NEG_PAD, LANES), F32)] + [wide] * 4, size=40000000,
    )(head_row, pad, weights, scaled, head_grad)
    grad = call(
        functools.partial(owner_kernel, 8), "owners", shape((ROWS, LANES), F32),
        [SM, SM, VM, VM],
        [pltpu.VMEM((BUCKETS * LANES, LANES), F32)] + [wide] * 4, size=30000000,
    )(asked, slopes.reshape(BUCKETS * LANES), came.reshape(BUCKETS * LANES, LANES), part)
    relation_grad = jnp.sum(rel_parts.astype(F32), axis=0)
    return (loss.reshape(EDGES), grad, relation_grad)


def solution(mesh):
    in_specs = (
        P("bucket", "col"),
        P(None, "col"),
        P("bucket"),
        P("bucket"),
        P("bucket", None),
        P("bucket"),
        P("bucket", None),
    )
    out_specs = (P("bucket"), P("bucket", "col"), P("bucket", "col"))
    return jax.shard_map(body, mesh=mesh, in_specs=in_specs, out_specs=out_specs, check_vma=False)
```

time: 227 us -> 138 us (0.61)
  the two profiles are of different devices: /device:TPU:32 before, /device:TPU:8 now
where the time goes in v3:
time: 138 us
  Pallas kernels  127 us (92%)
  starting transfers between devices  8.07 us (6%)
    pallas_call x1, Pallas kernels, body(): call(functools.partial(forward_kernel, negatives), 'forward', (shape(bloc...  75.3 us
    pallas_call x1, Pallas kernels, body(): call(functools.partial(entity_kernel, 8, negatives), 'entities', shape((R...  16.1 us
    pallas_call x1, Pallas kernels, body(): call(functools.partial(owner_kernel, 8), 'owners', shape((ROWS, LANES), F...  13.5 us
    pallas_call x1, Pallas kernels, body(): call(slope_kernel, 'slopes', shape(lists, F32), [VM], flags, group=1)(slope)  11.8 us
    pallas_call x1, Pallas kernels, body(): call(functools.partial(edge_kernel, 8), 'edges', (shape((1, EDGES), F32),...  10.3 us
    all_to_all x1, starting transfers between devices, body(): lax.all_to_all(rel_local.reshape(BUCKETS, LANES, LANES), 'bucket', split_...  8.07 us
  transfers between devices with their start and end apart: 1, of which 0 were waited for; matrix products, arithmetic and copies ran while one was open for 0% of the time, Pallas kernels for 21%

profile of v3, /device:TPU:8, one launch (start us, length us, event | category | flops | bytes accessed | tf_op | source)
XLA Modules:
  0.0 137.7 jit_solution(10627980331788728228)
XLA Ops:
  0.6 0.7 pad_bitcast_fusion
  1.4 0.6 copy.12
  2.0 75.3 %forward.1 = (s32[16,1,128]{2,1,0:T(1,128)}, s32[32,1,128]{2,1,0:T(1,128)}, bf16[32,128,128]{2,1,0:T(8,128)(2,1)}, bf16[2048,128]{1,0:T(8,128)(2,1)}, bf16[2048,...) custom-call(s32[2048]{0:T(1024)} %head_ref.3, ...), custom_call_target="tpu_custom_call" | custom-call | flops 600000000 | bytes 40000000 | tf_op jit(solution)/shard_map/forward/pallas_call | solution.py:528
  77.3 10.3 %edges.1 = (f32[1,2048]{1,0:T(1,128)}, f32[2048,128]{1,0:T(8,128)}, bf16[4096,128]{1,0:T(8,128)(2,1)}, f32[32,1,128]{2,1,0:T(1,128)}, bf16[2048,128]{1,0:T(8,128)(2,1)}) custom-call(s32[2048]{0:T(1024)} %rel_ref.3, s32[16,1,128]{2,1,0:T(1,128)} %get-tuple-element.20.target_ref, f32[16,1,128]{2,1,0:T(1,128)} %get-tuple-element.21.positive_ref, ...), custom_call_target="tpu_custom_call" | custom-call | flops 1000000 | bytes 20000000 | tf_op jit(solution)/shard_map/edges/pallas_call | solution.py:549
  87.6 11.8 %slopes.1 = f32[32,1,128]{2,1,0:T(1,128)} custom-call(f32[32,1,128]{2,1,0:T(1,128)} %get-tuple-element.31.slope_ref), custom_call_target="tpu_custom_call" | custom-call | flops 1000000 | bytes 4000000 | tf_op jit(solution)/shard_map/slopes/pallas_call | solution.py:557
  99.3 8.1 %all-to-all-start = ((bf16[32,128,128]{2,1,0:T(8,128)(2,1)}), bf16[32,128,128]{2,1,0:T(8,128)(2,1)S(1)}, u32[]{:S(2)}, u32[]{:S(2)}) async-start(bf16[32,128,128]{2,1,0:T(8,128)(2,1)} %bitcast.16), calls=%async_computation | async-start | bytes 2097152 | tf_op jit(solution)/shard_map/all_to_all | solution.py:559
  107.4 16.1 %entities.1.part_ref = f32[8192,128]{1,0:T(8,128)} custom-call(s32[2048]{0:T(1024)} %head_ref.3, s32[4096]{0:T(1024)} %bitcast.18, bf16[2048,1024]{1,0:T(8,128)(2,1)} %bitcast.14, bf16[2048,128]{1,0:T(8,128)(2,1)} %get-tuple-element.33.scaled_ref, f32[2048,128]{1,0:T(8,128)} %get-tuple-element.34.head_grad_ref), custom_call_target="tpu_custom_call" | custom-call | flops 1000000 | bytes 40000000 | tf_op jit(solution)/shard_map/entities/pallas_call | solution.py:562
  123.5 13.5 %owners.1 = f32[8192,128]{1,0:T(8,128)} custom-call(s32[4096]{0:T(1024)} %bitcast.20, f32[4096]{0:T(1024)} %bitcast.19, bf16[4096,128]{1,0:T(8,128)(2,1)} %bitcast.15, f32[8192,128]{1,0:T(8,128)} %entities.1.part_ref), custom_call_target="tpu_custom_call" | custom-call | flops 1000000 | bytes 30000000 | tf_op jit(solution)/shard_map/owners/pallas_call | solution.py:567
  136.9 0.0 all-to-all-done
  136.9 0.8 convert_reduce_fusion
Async XLA Ops:
  99.3 37.6 %all-to-all-start = ((bf16[32,128,128]{2,1,0:T(8,128)(2,1)}), bf16[32,128,128]{2,1,0:T(8,128)(2,1)S(1)}, u32[]{:S(2)}, u32[]{:S(2)}) async-start(bf16[32,128,128]{2,1,0:T(8,128)(2,1)} %bitcast.16), calls=%async_computation | async-start | bytes 2097152 | tf_op jit(solution)/shard_map/all_to_all | solution.py:559

commit v4 on v3

v4 whole, which is shorter than its diff:
```python
import functools

import jax
import jax.numpy as jnp
from jax import lax
from jax.experimental import pallas as pl
from jax.experimental.pallas import tpu as pltpu
from jax.sharding import PartitionSpec as P

LANES = 128
SPAN = 512
NEG_PAD = 1024
ROWS = 8192
DUMP = 8192
RELS = 4096
EDGES = 2048
BUCKETS = 32
COLS = 8
UNROLL = 64
CHIPS = 4
F32 = jnp.float32
BF16 = jnp.bfloat16
VM = pl.BlockSpec(memory_space=pltpu.VMEM)
SM = pl.BlockSpec(memory_space=pltpu.SMEM)
NT = (((1,), (1,)), ((), ()))
TN = (((0,), (0,)), ((), ()))


def call(kernel, name, outs, ins, scratch=(), flops=1000000, size=4000000, group=None):
    remote = {} if group is None else dict(collective_id=group, has_side_effects=True)
    return pl.pallas_call(
        kernel,
        name=name,
        out_shape=outs,
        in_specs=ins,
        out_specs=jax.tree.map(lambda _: VM, outs),
        scratch_shapes=scratch,
        compiler_params=pltpu.CompilerParams(vmem_limit_bytes=56 << 20, **remote),
        cost_estimate=pl.CostEstimate(flops=flops, bytes_accessed=size, transcendentals=0),
    )


def shape(dims, kind):
    return jax.ShapeDtypeStruct(dims, kind)


def iota(dims, axis):
    return lax.broadcasted_iota(jnp.int32, dims, axis)


def to_column(row):
    size = row.shape[1]
    same = iota((size, size), 0) == iota((size, size), 1)
    return jnp.sum(jnp.where(same, row, 0.0), axis=1, keepdims=True)


def to_row(column):
    size = column.shape[0]
    same = iota((size, size), 0) == iota((size, size), 1)
    return jnp.sum(jnp.where(same, column, 0.0), axis=0, keepdims=True)


def swap_halves(value):
    return pltpu.roll(value, LANES // 2, 1)


def times(left, right):
    lane = iota(left.shape, 1)
    first = lane < LANES // 2
    turned = swap_halves(right)
    real = jnp.where(first, right, turned)
    imag = jnp.where(first, -turned, right)
    return left * real + swap_halves(left) * imag


def times_conj(left, right):
    lane = iota(left.shape, 1)
    first = lane < LANES // 2
    turned = swap_halves(right)
    real = jnp.where(first, right, turned)
    imag = jnp.where(first, turned, -right)
    return left * real + swap_halves(left) * imag


def greet(axis, count):
    me = lax.axis_index(axis)
    barrier = pltpu.get_barrier_semaphore()

    def tell(i, carry):
        peer = lax.rem(me + i, count)
        pl.semaphore_signal(barrier, inc=1, device_id={axis: peer},
                            device_id_type=pl.DeviceIdType.MESH)
        return carry

    lax.fori_loop(1, count, tell, 0)
    pl.semaphore_wait(barrier, count - 1)


def spread(axis, count, src, dst, send_sem, recv_sem):
    me = lax.axis_index(axis)

    def send(i, carry):
        peer = lax.rem(me + i, count)
        pltpu.make_async_remote_copy(
            src_ref=src.at[peer], dst_ref=dst.at[me], send_sem=send_sem, recv_sem=recv_sem,
            device_id={axis: peer}, device_id_type=pl.DeviceIdType.MESH).start()
        return carry

    lax.fori_loop(1, count, send, 0)


def settle(axis, count, src, dst, send_sem, recv_sem):
    me = lax.axis_index(axis)
    rest = pl.ds(0, count - 1)
    pltpu.make_async_remote_copy(
        src_ref=src.at[rest], dst_ref=dst.at[rest], send_sem=send_sem, recv_sem=recv_sem,
        device_id={axis: lax.rem(me + 1, count)}, device_id_type=pl.DeviceIdType.MESH).wait()


def load_table(table_ref, wide_ref, rows):
    wide_ref[0:rows, :] = table_ref[...].astype(F32)


def to(peers):
    return dict(device_id=peers, device_id_type=pl.DeviceIdType.MESH)


def forward_kernel(negatives, head_ref, rel_ref, neg_ref, owner_ref, row_ref, table_ref, rtable_ref,
                   asked_ref, came_ref, slopes_ref, loss_ref, head_grad_ref, rel_grad_ref,
                   neg_grad_ref,
                   wide, rwide, prod_wide, heads, rels, tails, raw, scaled, weights, tail_wide,
                   target, request, inverse, found, fetched, slots, pack, got, keep, send, other,
                   parts, stats, slope_out, asked_s, target_s, inverse_s,
                   local_sem, bucket_send, bucket_recv, pack_send, pack_recv, swap_send, swap_recv,
                   weight_send, weight_recv, near_send, near_recv, part_send, part_recv):
    me = lax.axis_index("bucket")
    place = lax.axis_index("col")
    chip, core = place // 2, lax.rem(place, 2)
    near = {"col": 2 * chip + (1 - core)}

    barrier = pltpu.get_barrier_semaphore()
    for axis, count in (("bucket", BUCKETS), ("col", COLS)):
        def tell(i, carry):
            peer = lax.rem(lax.axis_index(axis) + i, count)
            pl.semaphore_signal(barrier, inc=1, **to({axis: peer}))
            return carry

        lax.fori_loop(1, count, tell, 0)
    lower = (iota((LANES, LANES), 0) <= iota((LANES, LANES), 1)).astype(BF16)
    lane = iota((LANES, LANES), 1).astype(F32)
    before = jnp.zeros((BUCKETS, 1), F32)
    nothing = jnp.zeros((BUCKETS, LANES), F32)
    high, low, first, last = nothing, nothing, nothing, nothing
    for block in range(EDGES // LANES):
        at = slice(block * LANES, (block + 1) * LANES)
        owner = owner_ref[:, at]
        row = row_ref[:, at]
        mine = iota((BUCKETS, LANES), 0) == owner
        hit = mine.astype(F32).astype(BF16)
        count = jnp.dot(hit, lower, preferred_element_type=F32)
        ranks = jnp.where(mine, count + before - 1.0, 0.0)
        rank = jnp.sum(ranks, axis=0, keepdims=True).astype(jnp.int32)
        before = before + count[:, LANES - 1 : LANES]
        target[block] = jnp.clip(owner * LANES + rank, 0, BUCKETS * LANES - 1)
        slot = iota((LANES, LANES), 0) == rank

        def placed(values):
            spread_out = jnp.where(slot, values, 0.0).astype(BF16)
            return lax.dot_general(hit, spread_out, NT, preferred_element_type=F32)

        high = high + placed((row >> 7).astype(F32))
        low = low + placed((row & 127).astype(F32))
        first = first + float(block) * placed(jnp.ones((1, LANES), F32))
        last = last + placed(lane)
    used = iota((BUCKETS, LANES), 1).astype(F32) < before
    rows = jnp.where(used, high * 128.0 + low, float(DUMP)).astype(jnp.int32)
    edges = jnp.where(used, first * 128.0 + last, float(EDGES)).astype(jnp.int32)
    for owner in range(BUCKETS):
        request[owner] = jnp.clip(rows[owner : owner + 1, :], 0, DUMP)
        inverse[owner] = jnp.clip(edges[owner : owner + 1, :], 0, EDGES)

    pl.semaphore_wait(barrier, BUCKETS + COLS - 2)
    spread("bucket", BUCKETS, request, asked_ref, bucket_send.at[0], bucket_recv.at[0])
    copies = [pltpu.make_async_copy(target, target_s, local_sem.at[0]),
              pltpu.make_async_copy(inverse, inverse_s, local_sem.at[1])]
    for copy in copies:
        copy.start()
    asked_ref[me] = request[me]

    load_table(table_ref, wide, ROWS)
    load_table(rtable_ref, rwide, RELS)
    wide[ROWS : ROWS + 8, :] = jnp.zeros((8, LANES), F32)
    prod_wide[EDGES : EDGES + 8, :] = jnp.zeros((8, LANES), F32)

    def pack_copy(step):
        return pltpu.make_async_remote_copy(
            src_ref=pack.at[step], dst_ref=got.at[step], send_sem=pack_send.at[step],
            recv_sem=pack_recv.at[step], **to({"col": 2 * lax.rem(chip + step, CHIPS) + core}))

    def fill(step):
        span = lax.rem(chip + step, CHIPS)

        def edge_step(j, carry):
            base = pl.multiple_of(span * SPAN + j * UNROLL, UNROLL)
            head = jnp.concatenate(
                [wide[pl.ds(head_ref[base + r], 1), :] for r in range(UNROLL)], axis=0)
            rel = jnp.concatenate(
                [rwide[pl.ds(rel_ref[base + r], 1), :] for r in range(UNROLL)], axis=0)
            product = times(head, rel).astype(BF16)
            at = pl.ds(base, UNROLL)
            pack[step, pl.ds(pl.multiple_of(NEG_PAD + j * UNROLL, UNROLL), UNROLL), :] = product
            prod_wide[at, :] = product.astype(F32)
            heads[at, :] = head
            rels[at, :] = rel
            return carry

        lax.fori_loop(0, SPAN // UNROLL, edge_step, 0)

        def neg_step(j, carry):
            base = pl.multiple_of(j * UNROLL, UNROLL)
            start = span * NEG_PAD + j * UNROLL
            rows = jnp.concatenate(
                [wide[pl.ds(neg_ref[start + r], 1), :] for r in range(UNROLL)],
                axis=0).astype(BF16)
            pack[step, pl.ds(base, UNROLL), :] = rows
            return carry

        lax.fori_loop(0, NEG_PAD // UNROLL, neg_step, 0)

    fill(2)
    pack_copy(2).start()
    fill(1)
    pack_copy(1).start()
    settle("bucket", BUCKETS, request, asked_ref, bucket_send.at[0], bucket_recv.at[0])
    copy = pltpu.make_async_copy(asked_ref, asked_s, local_sem.at[2])
    copy.start()
    copy.wait()

    def bucket_copy(src, dst, which, peer):
        return pltpu.make_async_remote_copy(
            src_ref=src.at[peer], dst_ref=dst.at[me], send_sem=bucket_send.at[which],
            recv_sem=bucket_recv.at[which], **to({"bucket": peer}))

    def take(source, index, out, s):
        for part in range(LANES // UNROLL):
            rows = jnp.concatenate(
                [source[pl.ds(index[s, 0, part * UNROLL + r], 1), :] for r in range(UNROLL)],
                axis=0)
            out[s, part * UNROLL : (part + 1) * UNROLL, :] = rows.astype(BF16)

    def find(i, carry):
        peer = lax.rem(me + i, BUCKETS)
        take(wide, asked_s, found, peer)
        bucket_copy(found, fetched, 1, peer).start()
        return carry

    lax.fori_loop(1, BUCKETS, find, 0)
    take(wide, asked_s, fetched, me)

    fill(3)
    pack_copy(3).start()

    fill(0)

    for copy in copies:
        copy.wait()

    def give(i, carry):
        peer = lax.rem(me + i, BUCKETS)
        take(prod_wide, inverse_s, slots, peer)
        bucket_copy(slots, came_ref, 2, peer).start()
        return carry

    lax.fori_loop(1, BUCKETS, give, 0)
    take(prod_wide, inverse_s, came_ref, me)

    for step in range(1, CHIPS):
        pack_copy(step).wait()
    halves = SPAN // 2

    def swap(block):
        at = pl.ds(block * LANES, LANES)
        return pltpu.make_async_remote_copy(
            src_ref=send.at[at], dst_ref=other.at[at], send_sem=swap_send.at[block],
            recv_sem=swap_recv.at[block], **to(near))

    def score(half, out, block):
        at = pl.ds(pl.multiple_of(NEG_PAD + half * halves + block * LANES, LANES), LANES)
        parts_of = [pack.at[0]] + [got.at[step] for step in range(1, CHIPS)]
        left = jnp.concatenate([q[at, :] for q in parts_of], axis=1)

        def piece(i, carry):
            cut = pl.ds(pl.multiple_of(i * 256, 256), 256)
            right = jnp.concatenate([q[cut, :] for q in parts_of], axis=1)
            out[block * LANES : (block + 1) * LANES, cut] = lax.dot_general(
                left, right, NT, preferred_element_type=F32)
            return carry

        lax.fori_loop(0, NEG_PAD // 256, piece, 0)

    def source(step, side):
        return 2 * lax.rem(chip - step + CHIPS, CHIPS) + side

    def weight_copy(step, block, piece):
        ref = weights.at[piece, pl.ds(block * LANES, LANES)]
        flag = step * 2 + block
        return pltpu.make_async_remote_copy(
            src_ref=ref, dst_ref=ref, send_sem=weight_send.at[flag],
            recv_sem=weight_recv.at[flag],
            **to({"col": 2 * lax.rem(chip + step, CHIPS) + core}))

    def near_copy(step, block, side):
        ref = weights.at[source(step, side), pl.ds(block * LANES, LANES)]
        flag = step * 2 + block
        return pltpu.make_async_remote_copy(
            src_ref=ref, dst_ref=ref, send_sem=near_send.at[flag], recv_sem=near_recv.at[flag],
            **to(near))

    def blend(step, block, side):
        piece = source(step, side)
        at = pl.ds(pl.multiple_of(piece * halves + block * LANES, LANES), LANES)
        raw[at, :] = jnp.dot(weights[piece, block * LANES : (block + 1) * LANES, :],
                             pack[(CHIPS - step) % CHIPS, 0:NEG_PAD, :],
                             preferred_element_type=F32)

    for block in range(2):
        score(1 - core, send, block)
        swap(block).start()
    for block in range(2):
        score(core, keep, block)
    for block in range(2):
        swap(block).wait()
        at = slice(block * LANES, (block + 1) * LANES)
        scores = keep[at, :] + other[at, :]
        real = iota((LANES, NEG_PAD), 1) < negatives
        scores = jnp.where(real, scores, -jnp.inf)
        top = jnp.max(scores, axis=1, keepdims=True)
        expo = jnp.exp(scores - top)
        weights[place, at, :] = expo.astype(BF16)
        for step in (2, 1, 3):
            weight_copy(step, block, place).start()
        near_copy(0, block, core).start()
        stats[place, 0:1, at] = to_row(top)
        stats[place, 1:2, at] = to_row(jnp.sum(expo, axis=1, keepdims=True))

    settle("bucket", BUCKETS, found, fetched, bucket_send.at[1], bucket_recv.at[1])
    tail_wide[...] = fetched[...].reshape(BUCKETS * LANES, LANES).astype(F32)

    def tail_step(block, carry):
        base = pl.multiple_of(block * LANES, LANES)
        for part in range(LANES // UNROLL):
            rows = jnp.concatenate(
                [tail_wide[pl.ds(target_s[block, 0, part * UNROLL + r], 1), :]
                 for r in range(UNROLL)], axis=0)
            tails[pl.ds(pl.multiple_of(base + part * UNROLL, UNROLL), UNROLL), :] = rows
        at = pl.ds(base, LANES)
        both = tails[at, :] * prod_wide[at, :]
        parts[place, block] = to_row(jnp.sum(both, axis=1, keepdims=True))
        return carry

    lax.fori_loop(0, EDGES // LANES, tail_step, 0)

    def part_copy(k, ref, peer):
        return pltpu.make_async_remote_copy(
            src_ref=ref.at[place], dst_ref=ref.at[place], send_sem=part_send.at[k],
            recv_sem=part_recv.at[k], **to({"col": peer}))

    def tell_parts(i, carry):
        peer = lax.rem(place + i, COLS)
        part_copy(0, parts, peer).start()
        part_copy(1, stats, peer).start()
        return carry

    lax.fori_loop(1, COLS, tell_parts, 0)

    for block in range(2):
        blend(0, block, core)
    for block in range(2):
        near_copy(0, block, 1 - core).wait_recv()
        blend(0, block, 1 - core)
    for block in range(2):
        for step in (1, 3, 2):
            weight_copy(step, block, source(step, core)).wait_recv()
            near_copy(step, block, core).start()
            blend(step, block, core)
    rest = pl.ds(0, COLS - 1)
    for k, ref in enumerate((parts, stats)):
        pltpu.make_async_remote_copy(
            src_ref=ref.at[rest], dst_ref=ref.at[rest], send_sem=part_send.at[k],
            recv_sem=part_recv.at[k], **to(near)).wait()

    mass_of, slope_of = [], []
    deal = jnp.zeros((BUCKETS, LANES), F32)
    for block in range(EDGES // LANES):
        part, inner = block // 2, (block % 2) * LANES
        high = stats[part, 0:1, inner : inner + LANES]
        mass = stats[part, 1:2, inner : inner + LANES]
        positive = parts[0, block]
        for k in range(1, COLS):
            positive = positive + parts[k, block]
        top = jnp.maximum(high, positive)
        shrink = jnp.exp(high - top)
        expo = jnp.exp(positive - top)
        total = mass * shrink + expo
        slope = expo / total - 1.0
        loss_ref[block] = top + jnp.log(total) - positive
        mass_of.append(shrink / total)
        slope_of.append(slope)
        goal = target[block]
        hit = (iota((BUCKETS, LANES), 0) == (goal >> 7)).astype(F32).astype(BF16)
        slot = iota((LANES, LANES), 0) == (goal & 127)
        left_over = slope
        for _ in range(3):
            piece = left_over.astype(BF16)
            spread_out = jnp.where(slot, piece.astype(F32), 0.0).astype(BF16)
            deal = deal + lax.dot_general(hit, spread_out, NT, preferred_element_type=F32)
            left_over = left_over - piece.astype(F32)
    for owner in range(BUCKETS):
        slope_out[owner] = deal[owner : owner + 1, :]
    spread("bucket", BUCKETS, slope_out, slopes_ref, bucket_send.at[3], bucket_recv.at[3])
    slopes_ref[me] = slope_out[me]

    for block in range(2):
        for step in (1, 3, 2):
            near_copy(step, block, 1 - core).wait_recv()
            blend(step, block, 1 - core)
    for block in range(EDGES // LANES):
        at = slice(block * LANES, (block + 1) * LANES)
        scale = to_column(mass_of[block])
        scaled[at, :] = (prod_wide[at, :] * scale).astype(BF16)
        down = raw[at, :] * scale + to_column(slope_of[block]) * tails[at, :]
        head_grad_ref[at, :] = times_conj(down, rels[at, :])
        rel_grad_ref[at, :] = times_conj(down, heads[at, :])
    for span in range(CHIPS):
        total = jnp.zeros((NEG_PAD, LANES), F32)
        for side in range(2):
            piece = 2 * span + side
            total = total + lax.dot_general(
                weights[piece], scaled[piece * halves : (piece + 1) * halves, :], TN,
                preferred_element_type=F32)
        neg_grad_ref[span] = total
    for block in range(2):
        for step in range(CHIPS):
            near_copy(step, block, core).wait_send()
        for step in range(1, CHIPS):
            weight_copy(step, block, place).wait_send()
    settle("bucket", BUCKETS, slope_out, slopes_ref, bucket_send.at[3], bucket_recv.at[3])
    settle("bucket", BUCKETS, slots, came_ref, bucket_send.at[2], bucket_recv.at[2])


def relation_kernel(unroll, rel_ref, grad_ref, out_ref, a0, a1, a2, a3):
    sums = (a0, a1, a2, a3)
    for one in sums:
        one[...] = jnp.zeros_like(one)

    def step(j, carry):
        for r in range(unroll):
            for k, one in enumerate(sums):
                edge = k * SPAN + j * unroll + r
                place = pl.ds(rel_ref[edge], 1)
                one[place, :] = one[place, :] + grad_ref[pl.ds(edge, 1), :]
        return carry

    lax.fori_loop(0, SPAN // unroll, step, 0)
    out_ref[...] = ((a0[...] + a1[...]) + (a2[...] + a3[...])).astype(BF16)


def entity_kernel(unroll, negatives, head_ref, neg_ref, asked_ref, slope_ref, head_grad_ref,
                  neg_grad_ref, came_ref, out_ref, wide, a0, a1, a2, a3):
    sums = (a0, a1, a2, a3)
    for one in sums:
        one[...] = jnp.zeros_like(one)
    wide[...] = came_ref[...].astype(F32)

    def edge_step(j, carry):
        for r in range(unroll):
            for k, one in enumerate(sums):
                edge = k * SPAN + j * unroll + r
                place = pl.ds(head_ref[edge], 1)
                one[place, :] = one[place, :] + head_grad_ref[pl.ds(edge, 1), :]
        return carry

    lax.fori_loop(0, SPAN // unroll, edge_step, 0)

    def neg_step(j, carry):
        for r in range(unroll):
            for k, one in enumerate(sums):
                place = pl.ds(neg_ref[k * NEG_PAD + j * unroll + r], 1)
                one[place, :] = one[place, :] + neg_grad_ref[k, pl.ds(j * unroll + r, 1), :]
        return carry

    lax.fori_loop(0, negatives // unroll, neg_step, 0)
    each = BUCKETS // 4

    def source(s, carry):
        def group(j):
            for r in range(unroll):
                for k, one in enumerate(sums):
                    owner = k * each + s
                    slot = j * unroll + r
                    place = pl.ds(asked_ref[owner * LANES + slot], 1)
                    term = slope_ref[owner * LANES + slot] * wide[pl.ds(owner * LANES + slot, 1), :]
                    one[place, :] = one[place, :] + term
            return j + 1

        def more(j):
            at = jnp.minimum(j * unroll, LANES - 1)
            first = asked_ref[s * LANES + at]
            for k in range(1, 4):
                first = jnp.minimum(first, asked_ref[(k * each + s) * LANES + at])
            return jnp.logical_and(j * unroll < LANES, first < DUMP)

        lax.while_loop(more, group, 0)
        return carry

    lax.fori_loop(0, each, source, 0)
    total = (a0[0:ROWS, :] + a1[0:ROWS, :]) + (a2[0:ROWS, :] + a3[0:ROWS, :])
    out_ref[...] = total


def body(entity_table, relation_table, head_row, relation_id, tail_owner, tail_row, negative_row):
    negatives = negative_row.shape[1]
    pad = jnp.pad(negative_row, ((0, 0), (0, NEG_PAD - negatives)), constant_values=DUMP)
    pad = pad.reshape(CHIPS * NEG_PAD)
    wide = pltpu.VMEM((ROWS + 8, LANES), F32)
    lists = (BUCKETS, 1, LANES)
    blocks = (EDGES // LANES, 1, LANES)
    grid = (BUCKETS, LANES, LANES)
    half = pltpu.VMEM((SPAN // 2, NEG_PAD), F32)
    packs = pltpu.VMEM((CHIPS, NEG_PAD + SPAN, LANES), BF16)
    flag = pltpu.SemaphoreType.DMA
    flat32 = pltpu.VMEM((EDGES, LANES), F32)
    asked, came, slopes, loss, head_grad, rel_grad, neg_grad = call(
        functools.partial(forward_kernel, negatives), "forward",
        (shape(lists, jnp.int32), shape(grid, BF16), shape(lists, F32), shape(blocks, F32),
         shape((EDGES, LANES), F32), shape((EDGES, LANES), F32),
         shape((CHIPS, NEG_PAD, LANES), F32)),
        [SM] * 3 + [VM] * 4,
        [wide, pltpu.VMEM((RELS, LANES), F32), pltpu.VMEM((EDGES + 8, LANES), F32),
         flat32, flat32, flat32, flat32, pltpu.VMEM((EDGES, LANES), BF16),
         pltpu.VMEM((COLS, SPAN // 2, NEG_PAD), BF16),
         pltpu.VMEM((BUCKETS * LANES, LANES), F32), pltpu.VMEM(blocks, jnp.int32),
         pltpu.VMEM(lists, jnp.int32), pltpu.VMEM(lists, jnp.int32),
         pltpu.VMEM(grid, BF16), pltpu.VMEM(grid, BF16), pltpu.VMEM(grid, BF16),
         packs, packs, half, half, half,
         pltpu.VMEM((COLS,) + blocks, F32), pltpu.VMEM((COLS, 2, SPAN // 2), F32),
         pltpu.VMEM(lists, F32), pltpu.SMEM(lists, jnp.int32),
         pltpu.SMEM(blocks, jnp.int32), pltpu.SMEM(lists, jnp.int32),
         flag((3,)), flag((4,)), flag((4,)), flag((CHIPS,)), flag((CHIPS,)), flag((2,)),
         flag((2,)), flag((2 * CHIPS,)), flag((2 * CHIPS,)), flag((2 * CHIPS,)),
         flag((2 * CHIPS,)), flag((2,)), flag((2,))],
        flops=600000000, size=40000000, group=0,
    )(head_row, relation_id, pad, tail_owner.reshape(1, EDGES), tail_row.reshape(1, EDGES),
      entity_table, relation_table)

    rel_local = call(
        functools.partial(relation_kernel, 8), "relations", shape((RELS, LANES), BF16),
        [SM, VM], [pltpu.VMEM((RELS, LANES), F32)] * 4, size=10000000,
    )(relation_id, rel_grad)
    rel_parts = lax.all_to_all(rel_local.reshape(BUCKETS, LANES, LANES), "bucket",
                               split_axis=0, concat_axis=0, tiled=True)
    grad = call(
        functools.partial(entity_kernel, 8, negatives), "entities", shape((ROWS, LANES), F32),
        [SM] * 4 + [VM] * 3,
        [pltpu.VMEM((BUCKETS * LANES, LANES), F32)] + [wide] * 4, size=60000000,
    )(head_row, pad, asked.reshape(BUCKETS * LANES), slopes.reshape(BUCKETS * LANES), head_grad,
      neg_grad, came.reshape(BUCKETS * LANES, LANES))
    relation_grad = jnp.sum(rel_parts.astype(F32), axis=0)
    return (loss.reshape(EDGES), grad, relation_grad)


def solution(mesh):
    in_specs = (
        P("bucket", "col"),
        P(None, "col"),
        P("bucket"),
        P("bucket"),
        P("bucket", None),
        P("bucket"),
        P("bucket", None),
    )
    out_specs = (P("bucket"), P("bucket", "col"), P("bucket", "col"))
    return jax.shard_map(body, mesh=mesh, in_specs=in_specs, out_specs=out_specs, check_vma=False)
```

time: 138 us -> 118 us (0.86)
  the two profiles are of different devices: /device:TPU:8 before, /device:TPU:32 now
where the time goes in v4:
time: 118 us
  Pallas kernels  101 us (86%)
  waiting for transfers between devices  7.3 us (6%)
  starting transfers between devices  6.61 us (6%)
  local copies, waits for them, and re-layouts  1.94 us (2%)
    pallas_call x1, Pallas kernels, body(): call(functools.partial(forward_kernel, negatives), 'forward', (shape(list...  73.8 us
    pallas_call x1, Pallas kernels, body(): call(functools.partial(entity_kernel, 8, negatives), 'entities', shape((R...  20.9 us
    all_to_all x1, waiting for transfers between devices, body(): lax.all_to_all(rel_local.reshape(BUCKETS, LANES, LANES), 'bucket', split_...  7.3 us
    all_to_all x1, starting transfers between devices, body(): lax.all_to_all(rel_local.reshape(BUCKETS, LANES, LANES), 'bucket', split_...  6.61 us
    pallas_call x1, Pallas kernels, body(): call(functools.partial(relation_kernel, 8), 'relations', shape((RELS, LAN...  5.98 us
  transfers between devices with their start and end apart: 1, of which 1 were waited for; matrix products, arithmetic and copies ran while one was open for 0% of the time, Pallas kernels for 18%

profile of v4, /device:TPU:32, one launch (start us, length us, event | category | flops | bytes accessed | tf_op | source)
XLA Modules:
  0.0 117.9 jit_solution(8404448083478258312)
XLA Ops:
  0.6 0.7 pad_bitcast_fusion
  1.4 0.6 copy.12
  2.0 73.8 %forward.1 = (s32[32,1,128]{2,1,0:T(1,128)}, bf16[32,128,128]{2,1,0:T(8,128)(2,1)}, f32[32,1,128]{2,1,0:T(1,128)}, f32[16,1,128]{2,1,0:T(1,128)}, f32[2048,128]{...) custom-call(s32[2048]{0:T(1024)} %head_ref.3, s32[2048]{0:T(1024)} %rel_ref.3, s32[4096]{0:T(1024)} %bitcast.14, ...), custom_call_target="tpu_custom_call" | custom-call | flops 600000000 | bytes 40000000 | tf_op jit(solution)/shard_map/forward/pallas_call | solution.py:533
  75.7 6.0 %relations.1 = bf16[4096,128]{1,0:T(8,128)(2,1)} custom-call(s32[2048]{0:T(1024)} %rel_ref.3, f32[2048,128]{1,0:T(8,128)} %get-tuple-element.16.grad_ref), custom_call_target="tpu_custom_call" | custom-call | flops 1000000 | bytes 10000000 | tf_op jit(solution)/shard_map/relations/pallas_call | solution.py:556
  81.7 6.6 %all-to-all-start = ((bf16[32,128,128]{2,1,0:T(8,128)(2,1)}), bf16[32,128,128]{2,1,0:T(8,128)(2,1)S(1)}, u32[]{:S(2)}, u32[]{:S(2)}) async-start(bf16[32,128,128]{2,1,0:T(8,128)(2,1)} %bitcast.12), calls=%async_computation | async-start | bytes 2097152 | tf_op jit(solution)/shard_map/all_to_all | solution.py:560
  88.3 0.0 copy-start
  88.3 20.9 %entities.1 = f32[8192,128]{1,0:T(8,128)} custom-call(s32[2048]{0:T(1024)} %head_ref.3, s32[4096]{0:T(1024)} %bitcast.15, s32[4096]{0:T(1024)} %bitcast.16, f32[4096]{0:T(1024)} %bitcast.17, f32[2048,128]{1,0:T(8,128)} %get-tuple-element.13.head_grad_ref, f32[4,1024,128]{2,1,0:T(8,128)} %get-tuple-element.14.neg_grad_ref, bf16[4096,128]{1,0:T(8,128)(2,1)} %bitcast.13), custom_call_target="tpu_custom_call" | custom-call | flops 1000000 | bytes 60000000 | tf_op jit(solution)/shard_map/entities/pallas_call | solution.py:562
  109.2 7.3 %all-to-all-done = bf16[32,128,128]{2,1,0:T(8,128)(2,1)S(1)} async-done(((bf16[32,128,128]{2,1,0:T(8,128)(2,1)}), bf16[32,128,128]{2,1,0:T(8,128)(2,1)S(1)}, u32[]{:S(2)}, u32[]{:S(2)}) %all-to-all-start) | async-done | bytes 1048608 | tf_op jit(solution)/shard_map/all_to_all | solution.py:560
  116.5 0.8 convert_reduce_fusion
  117.3 0.0 copy-done
  117.3 0.6 copy.14
Async XLA Ops:
  81.7 34.8 %all-to-all-start = ((bf16[32,128,128]{2,1,0:T(8,128)(2,1)}), bf16[32,128,128]{2,1,0:T(8,128)(2,1)S(1)}, u32[]{:S(2)}, u32[]{:S(2)}) async-start(bf16[32,128,128]{2,1,0:T(8,128)(2,1)} %bitcast.12), calls=%async_computation | async-start | bytes 2097152 | tf_op jit(solution)/shard_map/all_to_all | solution.py:560
  88.3 29.0 %copy-start = (f32[16,1,128]{2,1,0:T(1,128)S(1)}, f32[16,1,128]{2,1,0:T(1,128)}, u32[]{:S(2)}) copy-start(f32[16,1,128]{2,1,0:T(1,128)} %get-tuple-element.10) | copy-start | bytes 24580

commit v5 on v4

--- a/solution.py
+++ b/solution.py
@@ -128,9 +128,9 @@
 def forward_kernel(negatives, head_ref, rel_ref, neg_ref, owner_ref, row_ref, table_ref, rtable_ref,
                    asked_ref, came_ref, slopes_ref, loss_ref, head_grad_ref, rel_grad_ref,
                    neg_grad_ref,
-                   wide, rwide, prod_wide, heads, rels, tails, raw, scaled, weights, tail_wide,
+                   wide, rwide, prod_wide, heads, rels, tails, raw, weights, tail_wide,
                    target, request, inverse, found, fetched, slots, pack, got, keep, send, other,
-                   parts, stats, slope_out, asked_s, target_s, inverse_s,
+                   parts, stats, slope_out, masses, tilts, asked_s, target_s, inverse_s,
                    local_sem, bucket_send, bucket_recv, pack_send, pack_recv, swap_send, swap_recv,
                    weight_send, weight_recv, near_send, near_recv, part_send, part_recv):
     me = lax.axis_index("bucket")
@@ -147,10 +147,9 @@
 
         lax.fori_loop(1, count, tell, 0)
     lower = (iota((LANES, LANES), 0) <= iota((LANES, LANES), 1)).astype(BF16)
-    lane = iota((LANES, LANES), 1).astype(F32)
     before = jnp.zeros((BUCKETS, 1), F32)
-    nothing = jnp.zeros((BUCKETS, LANES), F32)
-    high, low, first, last = nothing, nothing, nothing, nothing
+    high = jnp.zeros((BUCKETS, LANES), F32)
+    low = jnp.zeros((BUCKETS, LANES), F32)
     for block in range(EDGES // LANES):
         at = slice(block * LANES, (block + 1) * LANES)
         owner = owner_ref[:, at]
@@ -170,21 +169,15 @@
 
         high = high + placed((row >> 7).astype(F32))
         low = low + placed((row & 127).astype(F32))
-        first = first + float(block) * placed(jnp.ones((1, LANES), F32))
-        last = last + placed(lane)
     used = iota((BUCKETS, LANES), 1).astype(F32) < before
     rows = jnp.where(used, high * 128.0 + low, float(DUMP)).astype(jnp.int32)
-    edges = jnp.where(used, first * 128.0 + last, float(EDGES)).astype(jnp.int32)
     for owner in range(BUCKETS):
         request[owner] = jnp.clip(rows[owner : owner + 1, :], 0, DUMP)
-        inverse[owner] = jnp.clip(edges[owner : owner + 1, :], 0, EDGES)
 
     pl.semaphore_wait(barrier, BUCKETS + COLS - 2)
     spread("bucket", BUCKETS, request, asked_ref, bucket_send.at[0], bucket_recv.at[0])
-    copies = [pltpu.make_async_copy(target, target_s, local_sem.at[0]),
-              pltpu.make_async_copy(inverse, inverse_s, local_sem.at[1])]
-    for copy in copies:
-        copy.start()
+    target_copy = pltpu.make_async_copy(target, target_s, local_sem.at[0])
+    target_copy.start()
     asked_ref[me] = request[me]
 
     load_table(table_ref, wide, ROWS)
@@ -218,14 +211,20 @@
 
         def neg_step(j, carry):
             base = pl.multiple_of(j * UNROLL, UNROLL)
-            start = span * NEG_PAD + j * UNROLL
+            start = span * negatives + j * UNROLL
             rows = jnp.concatenate(
                 [wide[pl.ds(neg_ref[start + r], 1), :] for r in range(UNROLL)],
                 axis=0).astype(BF16)
             pack[step, pl.ds(base, UNROLL), :] = rows
             return carry
 
-        lax.fori_loop(0, NEG_PAD // UNROLL, neg_step, 0)
+        whole = negatives // UNROLL
+        lax.fori_loop(0, whole, neg_step, 0)
+        rest = negatives - whole * UNROLL
+        start = span * negatives + whole * UNROLL
+        rows = [wide[pl.ds(neg_ref[start + r], 1), :] for r in range(rest)]
+        rows.append(jnp.zeros((NEG_PAD - negatives, LANES), F32))
+        pack[step, whole * UNROLL : NEG_PAD, :] = jnp.concatenate(rows, axis=0).astype(BF16)
 
     fill(2)
     pack_copy(2).start()
@@ -262,8 +261,24 @@
 
     fill(0)
 
-    for copy in copies:
-        copy.wait()
+    lane = iota((LANES, LANES), 1).astype(F32)
+    edges = jnp.zeros((BUCKETS, LANES), F32)
+    for block in range(EDGES // LANES):
+        goal = target[block]
+        hit = (iota((BUCKETS, LANES), 0) == (goal >> 7)).astype(F32).astype(BF16)
+        slot = iota((LANES, LANES), 0) == (goal & 127)
+        one = jnp.where(slot, 1.0, 0.0).astype(BF16)
+        inner = jnp.where(slot, lane, 0.0).astype(BF16)
+        edges = (edges + lax.dot_general(hit, inner, NT, preferred_element_type=F32)
+                 + float(block * LANES) * lax.dot_general(
+                     hit, one, NT, preferred_element_type=F32))
+    edges = jnp.where(used, edges, float(EDGES)).astype(jnp.int32)
+    for owner in range(BUCKETS):
+        inverse[owner] = jnp.clip(edges[owner : owner + 1, :], 0, EDGES)
+    inverse_copy = pltpu.make_async_copy(inverse, inverse_s, local_sem.at[1])
+    inverse_copy.start()
+    inverse_copy.wait()
+    target_copy.wait()
 
     def give(i, carry):
         peer = lax.rem(me + i, BUCKETS)
@@ -322,6 +337,25 @@
         raw[at, :] = jnp.dot(weights[piece, block * LANES : (block + 1) * LANES, :],
                              pack[(CHIPS - step) % CHIPS, 0:NEG_PAD, :],
                              preferred_element_type=F32)
+
+    def publish(block):
+        for step in (2, 1, 3):
+            weight_copy(step, block, place).start()
+        near_copy(0, block, core).start()
+
+    def finish(step, block, side):
+        blend(step, block, side)
+        piece = source(step, side)
+        span = piece // 2
+        at = pl.ds(pl.multiple_of(piece * halves + block * LANES, LANES), LANES)
+        scale = to_column(masses[piece * 2 + block])
+        scaled = (prod_wide[at, :] * scale).astype(BF16)
+        down = raw[at, :] * scale + to_column(tilts[piece * 2 + block]) * tails[at, :]
+        head_grad_ref[at, :] = times_conj(down, rels[at, :])
+        rel_grad_ref[at, :] = times_conj(down, heads[at, :])
+        neg_grad_ref[span] = neg_grad_ref[span] + lax.dot_general(
+            weights[piece, block * LANES : (block + 1) * LANES, :], scaled, TN,
+            preferred_element_type=F32)
 
     for block in range(2):
         score(1 - core, send, block)
@@ -337,9 +371,8 @@
         top = jnp.max(scores, axis=1, keepdims=True)
         expo = jnp.exp(scores - top)
         weights[place, at, :] = expo.astype(BF16)
-        for step in (2, 1, 3):
-            weight_copy(step, block, place).start()
-        near_copy(0, block, core).start()
+        if block == 0:
+            publish(block)
         stats[place, 0:1, at] = to_row(top)
         stats[place, 1:2, at] = to_row(jnp.sum(expo, axis=1, keepdims=True))
 
@@ -373,23 +406,17 @@
 
     lax.fori_loop(1, COLS, tell_parts, 0)
 
-    for block in range(2):
-        blend(0, block, core)
-    for block in range(2):
-        near_copy(0, block, 1 - core).wait_recv()
-        blend(0, block, 1 - core)
-    for block in range(2):
-        for step in (1, 3, 2):
-            weight_copy(step, block, source(step, core)).wait_recv()
-            near_copy(step, block, core).start()
-            blend(step, block, core)
+    publish(1)
+    neg_grad_ref[...] = jnp.zeros_like(neg_grad_ref)
+    for step in (1, 3, 2):
+        weight_copy(step, 0, source(step, core)).wait_recv()
+        near_copy(step, 0, core).start()
     rest = pl.ds(0, COLS - 1)
     for k, ref in enumerate((parts, stats)):
         pltpu.make_async_remote_copy(
             src_ref=ref.at[rest], dst_ref=ref.at[rest], send_sem=part_send.at[k],
             recv_sem=part_recv.at[k], **to(near)).wait()
 
-    mass_of, slope_of = [], []
     deal = jnp.zeros((BUCKETS, LANES), F32)
     for block in range(EDGES // LANES):
         part, inner = block // 2, (block % 2) * LANES
@@ -404,8 +431,8 @@
         total = mass * shrink + expo
         slope = expo / total - 1.0
         loss_ref[block] = top + jnp.log(total) - positive
-        mass_of.append(shrink / total)
-        slope_of.append(slope)
+        masses[block] = shrink / total
+        tilts[block] = slope
         goal = target[block]
         hit = (iota((BUCKETS, LANES), 0) == (goal >> 7)).astype(F32).astype(BF16)
         slot = iota((LANES, LANES), 0) == (goal & 127)
@@ -420,25 +447,23 @@
     spread("bucket", BUCKETS, slope_out, slopes_ref, bucket_send.at[3], bucket_recv.at[3])
     slopes_ref[me] = slope_out[me]
 
+    finish(0, 0, core)
+    finish(0, 1, core)
     for block in range(2):
-        for step in (1, 3, 2):
-            near_copy(step, block, 1 - core).wait_recv()
-            blend(step, block, 1 - core)
-    for block in range(EDGES // LANES):
-        at = slice(block * LANES, (block + 1) * LANES)
-        scale = to_column(mass_of[block])
-        scaled[at, :] = (prod_wide[at, :] * scale).astype(BF16)
-        down = raw[at, :] * scale + to_column(slope_of[block]) * tails[at, :]
-        head_grad_ref[at, :] = times_conj(down, rels[at, :])
-        rel_grad_ref[at, :] = times_conj(down, heads[at, :])
-    for span in range(CHIPS):
-        total = jnp.zeros((NEG_PAD, LANES), F32)
-        for side in range(2):
-            piece = 2 * span + side
-            total = total + lax.dot_general(
-                weights[piece], scaled[piece * halves : (piece + 1) * halves, :], TN,
-                preferred_element_type=F32)
-        neg_grad_ref[span] = total
+        near_copy(0, block, 1 - core).wait_recv()
+        finish(0, block, 1 - core)
+    for step in (1, 3, 2):
+        finish(step, 0, core)
+    for step in (1, 3, 2):
+        near_copy(step, 0, 1 - core).wait_recv()
+        finish(step, 0, 1 - core)
+    for step in (1, 3, 2):
+        weight_copy(step, 1, source(step, core)).wait_recv()
+        near_copy(step, 1, core).start()
+        finish(step, 1, core)
+    for step in (1, 3, 2):
+        near_copy(step, 1, 1 - core).wait_recv()
+        finish(step, 1, 1 - core)
     for block in range(2):
         for step in range(CHIPS):
             near_copy(step, block, core).wait_send()
@@ -447,7 +472,6 @@
     settle("bucket", BUCKETS, slope_out, slopes_ref, bucket_send.at[3], bucket_recv.at[3])
     settle("bucket", BUCKETS, slots, came_ref, bucket_send.at[2], bucket_recv.at[2])
 
-
 def relation_kernel(unroll, rel_ref, grad_ref, out_ref, a0, a1, a2, a3):
     sums = (a0, a1, a2, a3)
     for one in sums:
@@ -485,7 +509,7 @@
     def neg_step(j, carry):
         for r in range(unroll):
             for k, one in enumerate(sums):
-                place = pl.ds(neg_ref[k * NEG_PAD + j * unroll + r], 1)
+                place = pl.ds(neg_ref[k * negatives + j * unroll + r], 1)
                 one[place, :] = one[place, :] + neg_grad_ref[k, pl.ds(j * unroll + r, 1), :]
         return carry
 
@@ -520,8 +544,7 @@
 
 def body(entity_table, relation_table, head_row, relation_id, tail_owner, tail_row, negative_row):
     negatives = negative_row.shape[1]
-    pad = jnp.pad(negative_row, ((0, 0), (0, NEG_PAD - negatives)), constant_values=DUMP)
-    pad = pad.reshape(CHIPS * NEG_PAD)
+    negs = negative_row.reshape(CHIPS * negatives)
     wide = pltpu.VMEM((ROWS + 8, LANES), F32)
     lists = (BUCKETS, 1, LANES)
     blocks = (EDGES // LANES, 1, LANES)
@@ -537,20 +560,21 @@
          shape((CHIPS, NEG_PAD, LANES), F32)),
         [SM] * 3 + [VM] * 4,
         [wide, pltpu.VMEM((RELS, LANES), F32), pltpu.VMEM((EDGES + 8, LANES), F32),
-         flat32, flat32, flat32, flat32, pltpu.VMEM((EDGES, LANES), BF16),
+         flat32, flat32, flat32, flat32,
          pltpu.VMEM((COLS, SPAN // 2, NEG_PAD), BF16),
          pltpu.VMEM((BUCKETS * LANES, LANES), F32), pltpu.VMEM(blocks, jnp.int32),
          pltpu.VMEM(lists, jnp.int32), pltpu.VMEM(lists, jnp.int32),
          pltpu.VMEM(grid, BF16), pltpu.VMEM(grid, BF16), pltpu.VMEM(grid, BF16),
          packs, packs, half, half, half,
          pltpu.VMEM((COLS,) + blocks, F32), pltpu.VMEM((COLS, 2, SPAN // 2), F32),
-         pltpu.VMEM(lists, F32), pltpu.SMEM(lists, jnp.int32),
+         pltpu.VMEM(lists, F32), pltpu.VMEM(blocks, F32), pltpu.VMEM(blocks, F32),
+         pltpu.SMEM(lists, jnp.int32),
          pltpu.SMEM(blocks, jnp.int32), pltpu.SMEM(lists, jnp.int32),
          flag((3,)), flag((4,)), flag((4,)), flag((CHIPS,)), flag((CHIPS,)), flag((2,)),
          flag((2,)), flag((2 * CHIPS,)), flag((2 * CHIPS,)), flag((2 * CHIPS,)),
          flag((2 * CHIPS,)), flag((2,)), flag((2,))],
         flops=600000000, size=40000000, group=0,
-    )(head_row, relation_id, pad, tail_owner.reshape(1, EDGES), tail_row.reshape(1, EDGES),
+    )(head_row, relation_id, negs, tail_owner.reshape(1, EDGES), tail_row.reshape(1, EDGES),
       entity_table, relation_table)
 
     rel_local = call(
@@ -563,7 +587,7 @@
         functools.partial(entity_kernel, 8, negatives), "entities", shape((ROWS, LANES), F32),
         [SM] * 4 + [VM] * 3,
         [pltpu.VMEM((BUCKETS * LANES, LANES), F32)] + [wide] * 4, size=60000000,
-    )(head_row, pad, asked.reshape(BUCKETS * LANES), slopes.reshape(BUCKETS * LANES), head_grad,
+    )(head_row, negs, asked.reshape(BUCKETS * LANES), slopes.reshape(BUCKETS * LANES), head_grad,
       neg_grad, came.reshape(BUCKETS * LANES, LANES))
     relation_grad = jnp.sum(rel_parts.astype(F32), axis=0)
     return (loss.reshape(EDGES), grad, relation_grad)

time: 118 us -> 114 us (0.966)
  Pallas kernels: 101 us -> 92.2 us
  waiting for transfers between devices: 7.3 us -> 10.8 us
    pallas_call x1, Pallas kernels: 20.9 us -> 16.6 us  [body(): call(functools.partial(entity_kernel, 8, negatives), 'entities', shape((R...]
    pallas_call x1, Pallas kernels: 73.8 us -> 69.6 us  [body(): call(functools.partial(forward_kernel, negatives), 'forward', (shape(list...]
    all_to_all x1, waiting for transfers between devices: 7.3 us -> 10.8 us  [body(): lax.all_to_all(rel_local.reshape(BUCKETS, LANES, LANES), 'bucket', split_...]
    reshape x0 -> x1, local copies, waits for them, and re-layouts: none -> 1.41 us  [body(): negs = negative_row.reshape(CHIPS * negatives)]
    unnamed x5 -> x3, local copies, waits for them, and re-layouts: 1.94 us -> 0.6 us
  transfers between devices with their start and end apart: 1 -> 1, of which waited for: 1 -> 1; matrix products, arithmetic and copies ran while one was open for 0% -> 0% of each run, Pallas kernels for 18% -> 15%
where the time goes in v5:
time: 114 us; the launch traced here: 113 us
  Pallas kernels  92.2 us (81%)
  waiting for transfers between devices  10.8 us (9%)
  starting transfers between devices  6.58 us (6%)
  local copies, waits for them, and re-layouts  2.01 us (2%)
    pallas_call x1, Pallas kernels, body(): call(functools.partial(forward_kernel, negatives), 'forward', (shape(list...  69.6 us
    pallas_call x1, Pallas kernels, body(): call(functools.partial(entity_kernel, 8, negatives), 'entities', shape((R...  16.6 us
    all_to_all x1, waiting for transfers between devices, body(): lax.all_to_all(rel_local.reshape(BUCKETS, LANES, LANES), 'bucket', split_...  10.8 us
    all_to_all x1, starting transfers between devices, body(): lax.all_to_all(rel_local.reshape(BUCKETS, LANES, LANES), 'bucket', split_...  6.58 us
    pallas_call x1, Pallas kernels, body(): call(functools.partial(relation_kernel, 8), 'relations', shape((RELS, LAN...  5.98 us
  transfers between devices with their start and end apart: 1, of which 1 were waited for; matrix products, arithmetic and copies ran while one was open for 0% of the time, Pallas kernels for 15%

profile of v5, /device:TPU:32, one launch (start us, length us, event | category | flops | bytes accessed | tf_op | source)
XLA Modules:
  0.0 113.0 jit_solution(17611391449635607353)
XLA Ops:
  0.6 1.4 %reshape.30.neg_ref = s32[4000]{0:T(1024)} reshape(s32[4,1000]{1,0:T(4,128)} %param.13) | data formatting | bytes 32000 | tf_op jit(solution)/shard_map/reshape | solution.py:547
  2.0 69.6 %forward.1 = (s32[32,1,128]{2,1,0:T(1,128)}, bf16[32,128,128]{2,1,0:T(8,128)(2,1)}, f32[32,1,128]{2,1,0:T(1,128)}, f32[16,1,128]{2,1,0:T(1,128)}, f32[2048,128]{...) custom-call(s32[2048]{0:T(1024)} %head_ref.3, s32[2048]{0:T(1024)} %rel_ref.3, s32[4000]{0:T(1024)} %reshape.30.neg_ref, ...), custom_call_target="tpu_custom_call" | custom-call | flops 600000000 | bytes 40000000 | tf_op jit(solution)/shard_map/forward/pallas_call | solution.py:556
  71.6 6.0 %relations.1 = bf16[4096,128]{1,0:T(8,128)(2,1)} custom-call(s32[2048]{0:T(1024)} %rel_ref.3, f32[2048,128]{1,0:T(8,128)} %get-tuple-element.16.grad_ref), custom_call_target="tpu_custom_call" | custom-call | flops 1000000 | bytes 10000000 | tf_op jit(solution)/shard_map/relations/pallas_call | solution.py:580
  77.6 6.6 %all-to-all-start = ((bf16[32,128,128]{2,1,0:T(8,128)(2,1)}), bf16[32,128,128]{2,1,0:T(8,128)(2,1)S(1)}, u32[]{:S(2)}, u32[]{:S(2)}) async-start(bf16[32,128,128]{2,1,0:T(8,128)(2,1)} %bitcast.7), calls=%async_computation | async-start | bytes 2097152 | tf_op jit(solution)/shard_map/all_to_all | solution.py:584
  84.2 0.0 copy-start
  84.2 16.6 %entities.1 = f32[8192,128]{1,0:T(8,128)} custom-call(s32[2048]{0:T(1024)} %head_ref.3, s32[4000]{0:T(1024)} %reshape.30.neg_ref, s32[4096]{0:T(1024)} %bitcast.9, f32[4096]{0:T(1024)} %bitcast.10, f32[2048,128]{1,0:T(8,128)} %get-tuple-element.13.head_grad_ref, f32[4,1024,128]{2,1,0:T(8,128)} %get-tuple-element.14.neg_grad_ref, bf16[4096,128]{1,0:T(8,128)(2,1)} %bitcast.8), custom_call_target="tpu_custom_call" | custom-call | flops 1000000 | bytes 60000000 | tf_op jit(solution)/shard_map/entities/pallas_call | solution.py:586
  100.8 10.8 %all-to-all-done = bf16[32,128,128]{2,1,0:T(8,128)(2,1)S(1)} async-done(((bf16[32,128,128]{2,1,0:T(8,128)(2,1)}), bf16[32,128,128]{2,1,0:T(8,128)(2,1)S(1)}, u32[]{:S(2)}, u32[]{:S(2)}) %all-to-all-start) | async-done | bytes 1048608 | tf_op jit(solution)/shard_map/all_to_all | solution.py:584
  111.6 0.8 convert_reduce_fusion
  112.4 0.0 copy-done
  112.4 0.6 copy.11
Async XLA Ops:
  77.6 34.0 %all-to-all-start = ((bf16[32,128,128]{2,1,0:T(8,128)(2,1)}), bf16[32,128,128]{2,1,0:T(8,128)(2,1)S(1)}, u32[]{:S(2)}, u32[]{:S(2)}) async-start(bf16[32,128,128]{2,1,0:T(8,128)(2,1)} %bitcast.7), calls=%async_computation | async-start | bytes 2097152 | tf_op jit(solution)/shard_map/all_to_all | solution.py:584
  84.2 28.2 %copy-start = (f32[16,1,128]{2,1,0:T(1,128)S(1)}, f32[16,1,128]{2,1,0:T(1,128)}, u32[]{:S(2)}) copy-start(f32[16,1,128]{2,1,0:T(1,128)} %get-tuple-element.10) | copy-start | bytes 24580

commit v6 on v5

--- a/solution.py
+++ b/solution.py
@@ -16,7 +16,7 @@
 EDGES = 2048
 BUCKETS = 32
 COLS = 8
-UNROLL = 64
+UNROLL = 128
 CHIPS = 4
 F32 = jnp.float32
 BF16 = jnp.bfloat16
@@ -578,7 +578,7 @@
       entity_table, relation_table)
 
     rel_local = call(
-        functools.partial(relation_kernel, 8), "relations", shape((RELS, LANES), BF16),
+        functools.partial(relation_kernel, 16), "relations", shape((RELS, LANES), BF16),
         [SM, VM], [pltpu.VMEM((RELS, LANES), F32)] * 4, size=10000000,
     )(relation_id, rel_grad)
     rel_parts = lax.all_to_all(rel_local.reshape(BUCKETS, LANES, LANES), "bucket",

time: 114 us -> 113 us (level)
  no operation moved by 1% of the time
where the time goes in v6:
time: 113 us
  Pallas kernels  92.5 us (82%)
  waiting for transfers between devices  10.4 us (9%)
  starting transfers between devices  6.24 us (6%)
  local copies, waits for them, and re-layouts  2.01 us (2%)
    pallas_call x1, Pallas kernels, body(): call(functools.partial(forward_kernel, negatives), 'forward', (shape(list...  69.4 us
    pallas_call x1, Pallas kernels, body(): call(functools.partial(entity_kernel, 8, negatives), 'entities', shape((R...  17.2 us
    all_to_all x1, waiting for transfers between devices, body(): lax.all_to_all(rel_local.reshape(BUCKETS, LANES, LANES), 'bucket', split_...  10.4 us
    all_to_all x1, starting transfers between devices, body(): lax.all_to_all(rel_local.reshape(BUCKETS, LANES, LANES), 'bucket', split_...  6.24 us
    pallas_call x1, Pallas kernels, body(): call(functools.partial(relation_kernel, 16), 'relations', shape((RELS, LA...  5.91 us
  transfers between devices with their start and end apart: 1, of which 1 were waited for; matrix products, arithmetic and copies ran while one was open for 0% of the time, Pallas kernels for 15%

profile of v6, /device:TPU:32, one launch (start us, length us, event | category | flops | bytes accessed | tf_op | source)
XLA Modules:
  0.0 112.6 jit_solution(16947607495076634256)
XLA Ops:
  0.6 1.4 %reshape.30.neg_ref = s32[4000]{0:T(1024)} reshape(s32[4,1000]{1,0:T(4,128)} %param.13) | data formatting | bytes 32000 | tf_op jit(solution)/shard_map/reshape | solution.py:547
  2.0 69.4 %forward.1 = (s32[32,1,128]{2,1,0:T(1,128)}, bf16[32,128,128]{2,1,0:T(8,128)(2,1)}, f32[32,1,128]{2,1,0:T(1,128)}, f32[16,1,128]{2,1,0:T(1,128)}, f32[2048,128]{...) custom-call(s32[2048]{0:T(1024)} %head_ref.3, s32[2048]{0:T(1024)} %rel_ref.3, s32[4000]{0:T(1024)} %reshape.30.neg_ref, ...), custom_call_target="tpu_custom_call" | custom-call | flops 600000000 | bytes 40000000 | tf_op jit(solution)/shard_map/forward/pallas_call | solution.py:556
  71.4 5.9 %relations.1 = bf16[4096,128]{1,0:T(8,128)(2,1)} custom-call(s32[2048]{0:T(1024)} %rel_ref.3, f32[2048,128]{1,0:T(8,128)} %get-tuple-element.16.grad_ref), custom_call_target="tpu_custom_call" | custom-call | flops 1000000 | bytes 10000000 | tf_op jit(solution)/shard_map/relations/pallas_call | solution.py:580
  77.3 6.2 %all-to-all-start = ((bf16[32,128,128]{2,1,0:T(8,128)(2,1)}), bf16[32,128,128]{2,1,0:T(8,128)(2,1)S(1)}, u32[]{:S(2)}, u32[]{:S(2)}) async-start(bf16[32,128,128]{2,1,0:T(8,128)(2,1)} %bitcast.7), calls=%async_computation | async-start | bytes 2097152 | tf_op jit(solution)/shard_map/all_to_all | solution.py:584
  83.6 0.0 copy-start
  83.6 17.2 %entities.1 = f32[8192,128]{1,0:T(8,128)} custom-call(s32[2048]{0:T(1024)} %head_ref.3, s32[4000]{0:T(1024)} %reshape.30.neg_ref, s32[4096]{0:T(1024)} %bitcast.9, f32[4096]{0:T(1024)} %bitcast.10, f32[2048,128]{1,0:T(8,128)} %get-tuple-element.13.head_grad_ref, f32[4,1024,128]{2,1,0:T(8,128)} %get-tuple-element.14.neg_grad_ref, bf16[4096,128]{1,0:T(8,128)(2,1)} %bitcast.8), custom_call_target="tpu_custom_call" | custom-call | flops 1000000 | bytes 60000000 | tf_op jit(solution)/shard_map/entities/pallas_call | solution.py:586
  100.8 10.4 %all-to-all-done = bf16[32,128,128]{2,1,0:T(8,128)(2,1)S(1)} async-done(((bf16[32,128,128]{2,1,0:T(8,128)(2,1)}), bf16[32,128,128]{2,1,0:T(8,128)(2,1)S(1)}, u32[]{:S(2)}, u32[]{:S(2)}) %all-to-all-start) | async-done | bytes 1048608 | tf_op jit(solution)/shard_map/all_to_all | solution.py:584
  111.2 0.8 convert_reduce_fusion
  112.0 0.0 copy-done
  112.0 0.6 copy.11
Async XLA Ops:
  77.3 33.9 %all-to-all-start = ((bf16[32,128,128]{2,1,0:T(8,128)(2,1)}), bf16[32,128,128]{2,1,0:T(8,128)(2,1)S(1)}, u32[]{:S(2)}, u32[]{:S(2)}) async-start(bf16[32,128,128]{2,1,0:T(8,128)(2,1)} %bitcast.7), calls=%async_computation | async-start | bytes 2097152 | tf_op jit(solution)/shard_map/all_to_all | solution.py:584
  83.6 28.5 %copy-start = (f32[16,1,128]{2,1,0:T(1,128)S(1)}, f32[16,1,128]{2,1,0:T(1,128)}, u32[]{:S(2)}) copy-start(f32[16,1,128]{2,1,0:T(1,128)} %get-tuple-element.10) | copy-start | bytes 24580
